TPU v7x, 32 devices: a whole 2x2x4 slice. The times are simulated.
32 devices in a mesh: dp: 2 (over x), expert: 16 (over z, y, core).
Axes of the slice: x: 2, y: 2, z: 4, core: 2. Of those that a mesh axis runs over, the one named last changes fastest.
Arguments:
- tokens: bfloat16 [4096, 1536], P(('dp', 'expert')), may hold values from -6 to 6
- cotangent: bfloat16 [4096, 1536], P(('dp', 'expert')), may hold values from -6 to 6
- lengths: int32 [32, 5], P(('dp', 'expert')), may hold values from 1 to 64, 128 in all within a row
- routes: int32 [4096, 8], P(('dp', 'expert')), may hold values from 0 to 15, all different within a row; in each aligned block of 128 rows (0 to 127, 128 to 255, ...) at most 80 rows name the same one
- gain_attn: float32 [1536], P('dp'), may hold values from 0.5 to 1.5
- w_query: float32 [1536, 1536], P('dp'), may hold values from -0.5 to 0.5
- key_weight: float32 [1536, 512], P('dp'), may hold values from -0.5 to 0.5
- value_weight: float32 [1536, 512], P('dp'), may hold values from -0.15625 to 0.15625
- w_out: float32 [1536, 1536], P('dp'), may hold values from -0.75 to 0.75
- gain_moe: float32 [1536], P('dp'), may hold values from 0.5 to 1.5
- w_router: float32 [1536, 16], P('dp'), may hold values from -0.078125 to 0.078125
- w_gate: float32 [16, 1536, 512], P('expert', 'dp'), may hold values from -0.15625 to 0.15625
- w_up: float32 [16, 1536, 512], P('expert', 'dp'), may hold values from -0.15625 to 0.15625
- w_down: float32 [16, 512, 1536], P('expert', 'dp'), may hold values from -1 to 1
Outputs:
- mixed: bfloat16 [4096, 1536], P(('dp', 'expert'))
- d_tokens: float32 [4096, 1536], P(('dp', 'expert'))
- d_gain_attn: float32 [1536], P('dp')
- d_w_query: float32 [1536, 1536], P('dp')
- d_w_key: float32 [1536, 512], P('dp')
- d_w_value: float32 [1536, 512], P('dp')
- d_w_out: float32 [1536, 1536], P('dp')
- d_gain_moe: float32 [1536], P('dp')
- d_w_router: float32 [1536, 16], P('dp')
- d_w_gate: float32 [16, 1536, 512], P('expert', 'dp')
- d_w_up: float32 [16, 1536, 512], P('expert', 'dp')
- d_w_down: float32 [16, 512, 1536], P('expert', 'dp')
Inputs may be any that keep to these rules, and one draw needn't show every extreme that they name: In each row the first 4 entries are the lengths of a sequence's documents in order and the last is the padding at its end; each row sums to 128 and its largest entry is 64. `routes`: each row names 8 different experts. In each aligned block of 128 rows (one sequence) no expert is named more than 80 times, and in some blocks an expert is named exactly 80 times.
All inputs are finite; a program needn't handle non-finite values.
Results may differ from a plain program's by a relative error of at most 0.02.
The roundings to bfloat16 on the way count: a program that leaves them out, or rounds other values in their place, can miss the bound.
Values may be sent and summed in bfloat16 or wider, within the bound.
No kernel may reach another device: no remote copies, remote signals or barrier semaphores. Data moves between devices by JAX's collectives and lax.ppermute only.
A program may use at most 192 MiB of HBM per device.

v0:
```python
import math

import jax
import jax.numpy as jnp
from jax import lax
from jax.sharding import PartitionSpec as P

HEAD_DIMENSION = 64


norm_eps = 1e-06
score_scale = 0.015625
rope_base = 10000.0
mask_fill = -1e30


def narrow(tensor):
    return tensor.astype(jnp.bfloat16)


def matmul(left, right):
    return jnp.dot(left, right, preferred_element_type=jnp.float32)


def inner_sum(left, right):
    return lax.dot_general(
        left, right, (((0,), (0,)), ((), ())), preferred_element_type=jnp.float32
    )


def outer_back(left, right):
    return lax.dot_general(
        left, right, (((1,), (1,)), ((), ())), preferred_element_type=jnp.float32
    )


def apply_rotary(field_in, places, head_count, turn_sign):
    half_dim = HEAD_DIMENSION // 2
    inverse = rope_base ** (-jnp.arange(half_dim, dtype=jnp.float32) * 2.0 / HEAD_DIMENSION)
    angles = places.astype(jnp.float32)[:, None] * inverse[None, :]
    cosine = jnp.cos(angles)[:, None, :]
    sine_t = turn_sign * jnp.sin(angles)[:, None, :]
    shaped = field_in.reshape(field_in.shape[0], head_count, HEAD_DIMENSION)
    first_half = shaped[..., :half_dim]
    second = shaped[..., half_dim:]
    turned = jnp.concatenate(
        [first_half * cosine - second * sine_t, second * cosine + first_half * sine_t], -1
    )
    return turned.reshape(field_in.shape)


def layout(doc_lengths, length):
    pieces = doc_lengths.shape[0]
    doc_ends = jnp.cumsum(doc_lengths)
    starts = doc_ends - doc_lengths
    places = jnp.arange(length, dtype=jnp.int32)
    segment = jnp.sum((places[:, None] >= doc_ends[None, :]).astype(jnp.int32), 1)
    owned_by = segment[:, None] == jnp.arange(pieces, dtype=jnp.int32)[None, :]
    incoming_placement = places - jnp.sum(jnp.where(owned_by, starts[None, :], 0), 1)
    live_rows = segment < pieces - 1
    allowed = (
        (segment[:, None] == segment[None, :])
        & (places[None, :] <= places[:, None])
        & (live_rows[None, :] | (places[:, None] == places[None, :]))
    )
    return (incoming_placement, live_rows, allowed)


def slot_table(route_ids, experts, capacity):
    flat_ids = route_ids.reshape(-1)
    hit_table = (flat_ids[:, None] == jnp.arange(experts, dtype=jnp.int32)[None, :]).astype(
        jnp.int32
    )
    rank_in = jnp.sum((jnp.cumsum(hit_table, 0) - 1) * hit_table, 1)
    return (flat_ids * capacity + rank_in).reshape(route_ids.shape)


def norm_back(incoming, scaled, inverse, gain_row):
    scaled_grad = incoming * gain_row
    return (
        inverse * (scaled_grad - scaled * jnp.mean(scaled_grad * scaled, -1, keepdims=True)),
        jnp.sum(incoming * scaled, 0),
    )


def shards(
    tokens,
    cotangent,
    lengths,
    routes,
    gain_attn,
    w_query,
    key_weight,
    value_weight,
    w_out,
    gain_moe,
    w_router,
    w_gate,
    w_up,
    w_down,
):
    gathered = (
        lax.all_gather(narrow(gain_attn), "dp", axis=0, tiled=True),
        lax.all_gather(narrow(w_query), "dp", axis=0, tiled=True),
        lax.all_gather(narrow(key_weight), "dp", axis=0, tiled=True),
        lax.all_gather(narrow(value_weight), "dp", axis=0, tiled=True),
        lax.all_gather(narrow(w_out), "dp", axis=0, tiled=True),
        lax.all_gather(narrow(gain_moe), "dp", axis=0, tiled=True),
        lax.all_gather(narrow(w_router), "dp", axis=0, tiled=True),
        lax.all_gather(narrow(w_gate), "dp", axis=1, tiled=True),
        lax.all_gather(narrow(w_up), "dp", axis=1, tiled=True),
        lax.all_gather(narrow(w_down), "dp", axis=1, tiled=True),
    )
    (
        gain_one,
        query_full,
        key_full,
        value_full,
        out_full,
        gain_two,
        router_full,
        gate_full,
        up_full,
        down_full,
    ) = gathered
    length = tokens.shape[0]
    model_width = tokens.shape[1]
    head_count = query_full.shape[1] // HEAD_DIMENSION
    key_heads = key_full.shape[1] // HEAD_DIMENSION
    group_size = head_count // key_heads
    top_count = routes.shape[1]
    owners = lax.axis_size("expert")
    local_experts = w_gate.shape[0]
    experts = owners * local_experts
    capacity = length * top_count * 5 // (experts * 4)
    incoming_placement, live_rows, allowed = layout(lengths[0], length)
    gain_one_f = gain_one.astype(jnp.float32)
    gain_two_f = gain_two.astype(jnp.float32)
    stream = tokens.astype(jnp.float32)
    inverse_one = lax.rsqrt(jnp.mean(stream * stream, -1, keepdims=True) + norm_eps)
    scaled_one = stream * inverse_one
    normed_one = narrow(scaled_one * gain_one_f)
    query_unrotated = matmul(normed_one, query_full)
    key_unrotated = matmul(normed_one, key_full)
    value_projected = matmul(normed_one, value_full)
    query_matrix = narrow(
        apply_rotary(query_unrotated, incoming_placement, head_count, 1.0)
    ).reshape(length, key_heads, group_size, HEAD_DIMENSION)
    key_matrix = narrow(apply_rotary(key_unrotated, incoming_placement, key_heads, 1.0)).reshape(
        length, key_heads, HEAD_DIMENSION
    )
    value_matrix = narrow(value_projected).reshape(length, key_heads, HEAD_DIMENSION)

    def masked_scores():
        scores = score_scale * jnp.einsum(
            "sngh,tnh->ngst", query_matrix, key_matrix, preferred_element_type=jnp.float32
        )
        return jnp.where(allowed, scores, mask_fill)

    masked = masked_scores()
    peak_score = jnp.max(masked, -1, keepdims=True)
    log_total = peak_score + jnp.log(jnp.sum(jnp.exp(masked - peak_score), -1, keepdims=True))
    attention = jnp.exp(masked - log_total)
    context = jnp.einsum(
        "ngst,tnh->sngh", narrow(attention), value_matrix, preferred_element_type=jnp.float32
    ).reshape(length, head_count * HEAD_DIMENSION)
    attended = narrow(jnp.where(live_rows[:, None], context, 0.0))
    stream_mid = stream + matmul(attended, out_full)
    inverse_two = lax.rsqrt(jnp.mean(stream_mid * stream_mid, -1, keepdims=True) + norm_eps)
    scaled_two = stream_mid * inverse_two
    normed_two = narrow(scaled_two * gain_two_f)
    logits = matmul(normed_two, router_full)
    gate_weights = jax.nn.softmax(jnp.take_along_axis(logits, routes, 1), -1)
    gate_low = narrow(gate_weights)
    slot_ids = slot_table(routes, experts, capacity)
    columns = jnp.arange(experts * capacity, dtype=jnp.int32)
    matches = slot_ids[:, :, None] == columns[None, None, :]
    pick_table = narrow(jnp.any(matches, 1))
    weigh_table = jnp.sum(jnp.where(matches, gate_low[:, :, None], jnp.zeros((), jnp.bfloat16)), 1)
    expert_rows = narrow(inner_sum(pick_table, normed_two)).reshape(
        owners, local_experts, capacity, model_width
    )
    received = lax.all_to_all(expert_rows, "expert", split_axis=0, concat_axis=0, tiled=True)
    gate_pre = jnp.einsum("secd,edf->secf", received, gate_full, preferred_element_type=jnp.float32)
    up_pre = jnp.einsum("secd,edf->secf", received, up_full, preferred_element_type=jnp.float32)
    hidden = narrow(jax.nn.silu(gate_pre) * up_pre)
    result = narrow(
        jnp.einsum("secf,efd->secd", hidden, down_full, preferred_element_type=jnp.float32)
    )
    returned = lax.all_to_all(result, "expert", split_axis=0, concat_axis=0, tiled=True)
    returned = returned.reshape(experts * capacity, model_width)
    mixed = narrow(stream_mid + matmul(weigh_table, returned))
    upstream = cotangent.astype(jnp.float32)
    cot_low = narrow(upstream)
    slot_grad = inner_sum(pick_table, cot_low)
    slot_gate = jnp.sum(weigh_table.astype(jnp.float32), 0)
    result_grad = narrow(slot_gate[:, None] * slot_grad).reshape(
        owners, local_experts, capacity, model_width
    )
    gate_slot = jnp.sum(returned.astype(jnp.float32) * slot_grad, 1)
    gate_grad = gate_slot[slot_ids]
    chosen_grad = gate_weights * (gate_grad - jnp.sum(gate_weights * gate_grad, 1, keepdims=True))
    expert_ids = jnp.arange(experts, dtype=jnp.int32)
    logit_grad = narrow(
        jnp.sum(
            jnp.where(
                routes[:, :, None] == expert_ids[None, None, :], chosen_grad[:, :, None], 0.0
            ),
            1,
        )
    )
    arrived = lax.all_to_all(result_grad, "expert", split_axis=0, concat_axis=0, tiled=True)
    hidden_grad = jnp.einsum(
        "secd,efd->secf", arrived, down_full, preferred_element_type=jnp.float32
    )
    sigmoid_g = jax.nn.sigmoid(gate_pre)
    silu_gate = jax.nn.silu(gate_pre)
    gate_pre_grad = narrow(hidden_grad * up_pre * sigmoid_g * (1.0 + gate_pre * (1.0 - sigmoid_g)))
    up_pre_grad = narrow(hidden_grad * silu_gate)
    hidden = narrow(silu_gate * up_pre)
    down_local = jnp.einsum("secf,secd->efd", hidden, arrived, preferred_element_type=jnp.float32)
    gate_local = jnp.einsum(
        "secd,secf->edf", received, gate_pre_grad, preferred_element_type=jnp.float32
    )
    up_local = jnp.einsum(
        "secd,secf->edf", received, up_pre_grad, preferred_element_type=jnp.float32
    )
    row_grad = narrow(
        jnp.einsum("secf,edf->secd", gate_pre_grad, gate_full, preferred_element_type=jnp.float32)
        + jnp.einsum("secf,edf->secd", up_pre_grad, up_full, preferred_element_type=jnp.float32)
    )
    row_home = lax.all_to_all(row_grad, "expert", split_axis=0, concat_axis=0, tiled=True).reshape(
        experts * capacity, model_width
    )
    normed_two_grad = matmul(pick_table, row_home) + outer_back(logit_grad, router_full)
    router_local = inner_sum(normed_two, logit_grad)
    mid_grad, gain_two_local = norm_back(normed_two_grad, scaled_two, inverse_two, gain_two_f)
    mid_grad = upstream + mid_grad
    branch_grad = narrow(mid_grad)
    out_local = inner_sum(attended, branch_grad)
    context_grad = narrow(outer_back(branch_grad, out_full))
    context_grad = jnp.where(live_rows[:, None], context_grad, jnp.zeros((), jnp.bfloat16)).reshape(
        length, key_heads, group_size, HEAD_DIMENSION
    )
    attention = jnp.exp(masked_scores() - log_total)
    attention_grad = jnp.einsum(
        "sngh,tnh->ngst", context_grad, value_matrix, preferred_element_type=jnp.float32
    )
    value_grad = narrow(
        jnp.einsum(
            "ngst,sngh->tnh", narrow(attention), context_grad, preferred_element_type=jnp.float32
        ).reshape(length, key_heads * HEAD_DIMENSION)
    )
    score_grad = narrow(
        attention * (attention_grad - jnp.sum(attention * attention_grad, -1, keepdims=True))
    )
    query_grad = score_scale * jnp.einsum(
        "ngst,tnh->sngh", score_grad, key_matrix, preferred_element_type=jnp.float32
    )
    key_grad = score_scale * jnp.einsum(
        "ngst,sngh->tnh", score_grad, query_matrix, preferred_element_type=jnp.float32
    )
    query_pre_grad = narrow(
        apply_rotary(
            query_grad.reshape(length, head_count * HEAD_DIMENSION),
            incoming_placement,
            head_count,
            -1.0,
        )
    )
    key_pre_grad = narrow(
        apply_rotary(
            key_grad.reshape(length, key_heads * HEAD_DIMENSION),
            incoming_placement,
            key_heads,
            -1.0,
        )
    )
    query_local = inner_sum(normed_one, query_pre_grad)
    key_local = inner_sum(normed_one, key_pre_grad)
    value_local = inner_sum(normed_one, value_grad)
    normed_one_grad = (
        outer_back(query_pre_grad, query_full)
        + outer_back(key_pre_grad, key_full)
        + outer_back(value_grad, value_full)
    )
    input_grad, gain_one_local = norm_back(normed_one_grad, scaled_one, inverse_one, gain_one_f)
    input_grad = mid_grad + input_grad
    fsdp_size = lax.axis_size("dp")
    local_list = (
        gain_one_local,
        query_local,
        key_local,
        value_local,
        out_local,
        gain_two_local,
        router_local,
    )
    packed = jnp.concatenate([piece.reshape(fsdp_size, -1) for piece in local_list], 1)
    summed = lax.psum(
        lax.psum_scatter(packed.astype(jnp.bfloat16), "dp", scatter_dimension=0, tiled=True),
        "expert",
    ).astype(jnp.float32)
    flat_sum = summed.reshape(-1)
    shard_shapes = (
        gain_attn.shape,
        w_query.shape,
        key_weight.shape,
        value_weight.shape,
        w_out.shape,
        gain_moe.shape,
        w_router.shape,
    )
    pieces_out = []
    offset = 0
    for shard_shape in shard_shapes:
        amount = math.prod(shard_shape)
        pieces_out.append(flat_sum[offset : offset + amount].reshape(shard_shape))
        offset = offset + amount
    gate_sum, up_sum, down_sum = (
        lax.psum_scatter(
            gate_local.astype(jnp.bfloat16), "dp", scatter_dimension=1, tiled=True
        ).astype(jnp.float32),
        lax.psum_scatter(
            up_local.astype(jnp.bfloat16), "dp", scatter_dimension=1, tiled=True
        ).astype(jnp.float32),
        lax.psum_scatter(
            down_local.astype(jnp.bfloat16), "dp", scatter_dimension=1, tiled=True
        ).astype(jnp.float32),
    )
    return (
        mixed,
        input_grad,
        pieces_out[0],
        pieces_out[1],
        pieces_out[2],
        pieces_out[3],
        pieces_out[4],
        pieces_out[5],
        pieces_out[6],
        gate_sum,
        up_sum,
        down_sum,
    )


def solution(mesh):
    placed = (
        P(("dp", "expert"), None),
        P(("dp", "expert"), None),
        P(("dp", "expert"), None),
        P(("dp", "expert"), None),
        P("dp"),
        P("dp", None),
        P("dp", None),
        P("dp", None),
        P("dp", None),
        P("dp"),
        P("dp", None),
        P("expert", "dp", None),
        P("expert", "dp", None),
        P("expert", "dp", None),
    )
    return jax.shard_map(
        shards,
        mesh=mesh,
        in_specs=placed,
        out_specs=(
            P(("dp", "expert"), None),
            P(("dp", "expert"), None),
            P("dp"),
            P("dp", None),
            P("dp", None),
            P("dp", None),
            P("dp", None),
            P("dp"),
            P("dp", None),
            P("expert", "dp", None),
            P("expert", "dp", None),
            P("expert", "dp", None),
        ),
        check_vma=False,
    )
```

profile of v0, /device:TPU:0, one launch (start us, length us, event | category | flops | bytes accessed | tf_op | source)
XLA Modules:
  0.0 1409.6 jit_solution(11472920736039251406)
XLA Ops:
  19.4 5.2 all-gather.1
  42.2 27.4 %all-gather.12.cloned.1.call-done = bf16[1536,512]{1,0:T(8,128)(2,1)} async-done(((bf16[768,512]{1,0:T(8,128)(2,1)}), bf16[1536,512]{1,0:T(8,128)(2,1)}) %all-gather.12.cloned.1.call-update) | async-done | bytes 1572880 | tf_op jit(solution)/shard_map/all_gather | solution.py:105
  72.5 61.9 %all-gather.14.cloned.1.call-done = bf16[1536,1536]{1,0:T(8,128)(2,1)} async-done(((bf16[768,1536]{1,0:T(8,128)(2,1)}), bf16[1536,1536]{1,0:T(8,128)(2,1)}) %all-gather.14.cloned.1.call-update) | async-done | bytes 4718608 | tf_op jit(solution)/shard_map/all_gather | solution.py:104
  140.3 58.7 %all-gather.16.cloned.1.call-done = bf16[1536,1536]{1,0:T(8,128)(2,1)} async-done(((bf16[768,1536]{1,0:T(8,128)(2,1)}), bf16[1536,1536]{1,0:T(8,128)(2,1)}) %all-gather.16.cloned.1.call-update) | async-done | bytes 4718608 | tf_op jit(solution)/shard_map/all_gather | solution.py:107
  205.6 5.7 all-to-all-start
  219.1 22.4 %all-gather.20.cloned.1.call-done = bf16[1,1536,512]{2,1,0:T(8,128)(2,1)} async-done(((bf16[1,768,512]{2,1,0:T(8,128)(2,1)}), bf16[1,1536,512]{2,1,0:T(8,128)(2,1)}) %all-gather.20.cloned.1.call-update) | async-done | bytes 1572880 | tf_op jit(solution)/shard_map/all_gather | solution.py:111
  241.5 42.9 %all-to-all-done = bf16[16,1,80,1536]{3,2,1,0:T(8,128)(2,1)} async-done(((bf16[16,1,80,1536]{3,2,1,0:T(8,128)(2,1)}), bf16[16,1,80,1536]{3,2,1,0:T(8,128)(2,1)}, u32[]{:S(2)}, u32[]{:S(2)}) %all-to-all-start) | async-done | bytes 3932192 | tf_op jit(solution)/shard_map/all_to_all | solution.py:183
  284.4 6.3 fusion.10
  300.1 5.9 fusion.14
  306.1 17.7 %all-to-all-start.1 = ((bf16[16,1,80,1536]{3,2,1,0:T(8,128)(2,1)}), bf16[16,1,80,1536]{3,2,1,0:T(8,128)(2,1)}, u32[]{:S(2)}, u32[]{:S(2)}) async-start(bf16[16,1,80,1536]{3,2,1,0:T(8,128)(2,1)} %fusion.14), calls=%async_computation.1 | async-start | bytes 7864320 | tf_op jit(solution)/shard_map/all_to_all | solution.py:190
  328.7 7.0 gather_fusion.1
  338.6 58.3 %all-to-all-done.1 = bf16[16,1,80,1536]{3,2,1,0:T(8,128)(2,1)} async-done(((bf16[16,1,80,1536]{3,2,1,0:T(8,128)(2,1)}), bf16[16,1,80,1536]{3,2,1,0:T(8,128)(2,1)}, u32[]{:S(2)}, u32[]{:S(2)}) %all-to-all-start.1) | async-done | bytes 3932192 | tf_op jit(solution)/shard_map/all_to_all | solution.py:190
  400.4 106.3 %all_to_all.20 = bf16[16,1,80,1536]{3,2,1,0:T(8,128)(2,1)S(1)} all-to-all(bf16[16,1,80,1536]{3,2,1,0:T(8,128)(2,1)S(1)} %bitcast.291), channel_id=1, replica_groups=mesh['dp'=2,'expert'=16] {'expert'}, dimensions={0} | all-to-all | bytes 7864320 | tf_op jit(solution)/shard_map/all_to_all | solution.py:212
  521.5 6.3 gather_fusion
  529.5 64.8 %all-to-all-done.3 = bf16[16,1,80,1536]{3,2,1,0:T(8,128)(2,1)} async-done(((bf16[16,1,80,1536]{3,2,1,0:T(8,128)(2,1)}), bf16[16,1,80,1536]{3,2,1,0:T(8,128)(2,1)}, u32[]{:S(2)}, u32[]{:S(2)}) %all-to-all-start.3) | async-done | bytes 3932192 | tf_op jit(solution)/shard_map/all_to_all | solution.py:232
  633.9 7.8 reshape.413
  641.7 7.9 reshape.410
  650.2 5.8 constant_dynamic-update-slice_fusion.5
  667.5 5.5 fusion.40
  673.4 5.9 fusion.37
  680.0 5.5 fusion.34
  685.6 282.9 %all-reduce.6.cloned.1.call-done = bf16[2,3159552]{1,0:T(2,128)(2,1)} async-done(((bf16[2,3159552]{1,0:T(2,128)(2,1)}), bf16[2,3159552]{1,0:T(2,128)(2,1)}) %all-reduce.6.cloned.1.call-update) | async-done | bytes 12638224
  968.5 16.4 %constant_dynamic-slice_fusion = bf16[1,3159552]{1,0:T(2,128)(2,1)} fusion(bf16[2,3159552]{1,0:T(2,128)(2,1)} %all-reduce.6.cloned.1.call-done, u32[]{:T(128)} %bitcast.91), kind=kLoop, calls=%fused_computation.175 | loop fusion | bytes 12638212
  989.4 8.2 reduce-scatter.8.cloned.1.call-done
  1000.1 26.4 %reduce-scatter.6.cloned.1.call-done = bf16[1,768,512]{2,1,0:T(8,128)(2,1)} async-done(((bf16[1,1536,512]{2,1,0:T(8,128)(2,1)}), bf16[1,768,512]{2,1,0:T(8,128)(2,1)}) %reduce-scatter.6.cloned.1.call-update) | async-done | bytes 786448 | tf_op jit(solution)/shard_map/reduce_scatter | solution.py:324
  1029.0 26.5 %reduce-scatter.4.cloned.1.call-done = bf16[1,768,512]{2,1,0:T(8,128)(2,1)} async-done(((bf16[1,1536,512]{2,1,0:T(8,128)(2,1)}), bf16[1,768,512]{2,1,0:T(8,128)(2,1)}) %reduce-scatter.4.cloned.1.call-update) | async-done | bytes 786448 | tf_op jit(solution)/shard_map/reduce_scatter | solution.py:321
  1059.1 235.8 %all-reduce.4.cloned.1.call-done = bf16[1,3159552]{1,0:T(2,128)(2,1)} async-done(((bf16[1,3159552]{1,0:T(2,128)(2,1)}), bf16[1,3159552]{1,0:T(2,128)(2,1)}) %all-reduce.4.cloned.1.call-update) | async-done | bytes 6319120 | tf_op jit(solution)/shard_map/psum | solution.py:300
  1294.9 14.8 %convert_element_type.250 = f32[1,3159552]{1,0:T(1,128)S(1)} convert(bf16[1,3159552]{1,0:T(2,128)(2,1)} %all-reduce.4.cloned.1.call-done) | non-fusion elementwise | flops 3159552 | bytes 18957312 | tf_op jit(solution)/shard_map/convert_element_type | solution.py:303
  1314.3 17.6 %slice_reduce_fusion.2 = (f32[393216]{0:T(1024)}, f32[393216]{0:T(1024)S(1)}) fusion(f32[1,3159552]{1,0:T(1,128)S(1)} %convert_element_type.250), kind=kLoop, calls=%fused_computation.64 | loop fusion | bytes 6291456 | tf_op jit(solution)/shard_map/slice | solution.py:318
  1331.8 54.3 %slice_reduce_fusion = (f32[1179648]{0:T(1024)}, f32[1179648]{0:T(1024)}) fusion(f32[1,3159552]{1,0:T(1,128)} %copy-done), kind=kLoop, calls=%fused_computation.11 | loop fusion | bytes 18874368 | tf_op jit(solution)/shard_map/slice | solution.py:318
  1387.0 5.8 reshape.419
  1396.7 5.8 reshape.416
  (290 shorter events, 164.4 us)
Async XLA Ops:
  7.2 33.0 %all-gather.10.cloned.1.call-start = ((), (), s32[]{:S(2)}) async-start(), calls=%async_computation.7 | async-start | bytes 2359296 | tf_op jit(solution)/shard_map/all_gather | solution.py:106
  9.8 59.8 %all-gather.12.cloned.1.call-start = ((), (), s32[]{:S(2)}) async-start(), calls=%async_computation.8 | async-start | bytes 2359296 | tf_op jit(solution)/shard_map/all_gather | solution.py:105
  10.8 123.6 %all-gather.14.cloned.1.call-start = ((), (), s32[]{:S(2)}) async-start(), calls=%async_computation.9 | async-start | bytes 7077888 | tf_op jit(solution)/shard_map/all_gather | solution.py:104
  15.0 184.1 %all-gather.16.cloned.1.call-start = ((), (), s32[]{:S(2)}) async-start(), calls=%async_computation.10 | async-start | bytes 7077888 | tf_op jit(solution)/shard_map/all_gather | solution.py:107
  19.0 15.1 %copy-start.53 = (s32[1,5]{1,0:T(1,128)S(1)}, s32[1,5]{1,0:T(1,128)}, u32[]{:S(2)}) copy-start(s32[1,5]{1,0:T(1,128)} %param.16) | copy-start | bytes 64
  19.0 16.3 %copy-start.1 = (bf16[128,1536]{1,0:T(8,128)(2,1)S(1)}, bf16[128,1536]{1,0:T(8,128)(2,1)}, u32[]{:S(2)}) copy-start(bf16[128,1536]{1,0:T(8,128)(2,1)} %param.14) | copy-start | bytes 1179652
  35.2 36.6 %copy-start.21 = (s32[128,8]{1,0:T(8,128)}, s32[128,8]{1,0:T(8,128)S(1)}, u32[]{:S(2)}) copy-start(s32[128,8]{1,0:T(8,128)S(1)} %copy.136) | copy-start | bytes 12292
  37.2 161.9 %copy-start.41 = (pred[128]{0:T(512)(128)(4,1)}, pred[128]{0:T(512)(128)(4,1)S(1)}, u32[]{:S(2)}) copy-start(pred[128]{0:T(512)(128)(4,1)S(1)} %broadcast_compare_fusion) | copy-start | bytes 388
  37.2 101.5 %copy-start.37 = (f32[128]{0:T(128)}, f32[128]{0:T(128)S(1)}, u32[]{:S(2)}) copy-start(f32[128]{0:T(128)S(1)} %add_rsqrt_fusion.1) | copy-start | bytes 1540
  38.7 100.1 %copy-start.29 = (f32[128,32]{0,1:T(8,128)}, f32[128,32]{0,1:T(8,128)S(1)}, u32[]{:S(2)}) copy-start(f32[128,32]{0,1:T(8,128)S(1)} %get-tuple-element.88) | copy-start | bytes 49156
  42.2 97.6 %copy-start.20 = (bf16[128,512]{0,1:T(8,128)(2,1)}, bf16[128,512]{0,1:T(8,128)(2,1)S(1)}, u32[]{:S(2)}) copy-start(bf16[128,512]{0,1:T(8,128)(2,1)S(1)} %copy.126) | copy-start | bytes 393220
  72.5 66.5 %copy-start.23 = (bf16[128,8,32]{0,2,1:T(8,128)(2,1)S(1)}, bf16[128,8,32]{0,2,1:T(8,128)(2,1)}, u32[]{:S(2)}) copy-start(bf16[128,8,32]{0,2,1:T(8,128)(2,1)} %get-tuple-element.84) | copy-start | bytes 196612
  139.7 62.6 %copy-start.27 = (f32[8,3,128]{2,1,0:T(4,128)}, f32[8,3,128]{2,1,0:T(4,128)S(1)}, u32[]{:S(2)}) copy-start(f32[8,3,128]{2,1,0:T(4,128)S(1)} %log_add_fusion) | copy-start | bytes 36868
  140.3 62.0 %copy-start.4 = (bf16[128,1536]{1,0:T(8,128)(2,1)}, bf16[128,1536]{1,0:T(8,128)(2,1)S(1)}, u32[]{:S(2)}) copy-start(bf16[128,1536]{1,0:T(8,128)(2,1)S(1)} %copy.130) | copy-start | bytes 1179652
  202.3 394.8 %copy-start.46 = (f32[128]{0:T(128)}, f32[128]{0:T(128)S(1)}, u32[]{:S(2)}) copy-start(f32[128]{0:T(128)S(1)} %add_rsqrt_fusion) | copy-start | bytes 1540
  205.6 78.8 %all-to-all-start = ((bf16[16,1,80,1536]{3,2,1,0:T(8,128)(2,1)}), bf16[16,1,80,1536]{3,2,1,0:T(8,128)(2,1)}, u32[]{:S(2)}, u32[]{:S(2)}) async-start(bf16[16,1,80,1536]{3,2,1,0:T(8,128)(2,1)} %bitcast.290), calls=%async_computation | async-start | bytes 7864320 | tf_op jit(solution)/shard_map/all_to_all | solution.py:183
  211.3 30.2 %all-gather.20.cloned.1.call-start = ((), (), s32[]{:S(2)}) async-start(), calls=%async_computation.12 | async-start | bytes 2359296 | tf_op jit(solution)/shard_map/all_gather | solution.py:111
  213.8 76.9 %all-gather.18.cloned.1.call-start = ((), (), s32[]{:S(2)}) async-start(), calls=%async_computation.11 | async-start | bytes 2359296 | tf_op jit(solution)/shard_map/all_gather | solution.py:110
  216.2 83.9 %all-gather.22.cloned.1.call-start = ((), (), s32[]{:S(2)}) async-start(), calls=%async_computation.13 | async-start | bytes 2359296 | tf_op jit(solution)/shard_map/all_gather | solution.py:112
  306.1 17.8 %copy-start.36 = (f32[768,16]{0,1:T(8,128)S(1)}, f32[768,16]{0,1:T(8,128)}, u32[]{:S(2)}) copy-start(f32[768,16]{0,1:T(8,128)} %param.24) | copy-start | bytes 147460
  306.1 90.9 %all-to-all-start.1 = ((bf16[16,1,80,1536]{3,2,1,0:T(8,128)(2,1)}), bf16[16,1,80,1536]{3,2,1,0:T(8,128)(2,1)}, u32[]{:S(2)}, u32[]{:S(2)}) async-start(bf16[16,1,80,1536]{3,2,1,0:T(8,128)(2,1)} %fusion.14), calls=%async_computation.1 | async-start | bytes 7864320 | tf_op jit(solution)/shard_map/all_to_all | solution.py:190
  400.4 106.4 %copy-start.13 = (f32[16,80,512]{2,1,0:T(8,128)S(1)}, f32[16,80,512]{2,1,0:T(8,128)}, u32[]{:S(2)}) copy-start(f32[16,80,512]{2,1,0:T(8,128)} %fusion.10) | copy-start | bytes 7864324
  400.4 106.4 %copy-start.15 = (f32[16,80,512]{2,1,0:T(8,128)S(1)}, f32[16,80,512]{2,1,0:T(8,128)}, u32[]{:S(2)}) copy-start(f32[16,80,512]{2,1,0:T(8,128)} %copy-done.14) | copy-start | bytes 7864324
  400.4 106.4 %copy-start.52 = (bf16[1,512,1536]{2,1,0:T(8,128)(2,1)S(1)}, bf16[1,512,1536]{2,1,0:T(8,128)(2,1)}, u32[]{:S(2)}) copy-start(bf16[1,512,1536]{2,1,0:T(8,128)(2,1)} %all-gather.22.cloned.1.call-done) | copy-start | bytes 4718596
  516.6 77.7 %all-to-all-start.3 = ((bf16[16,1,80,1536]{3,2,1,0:T(8,128)(2,1)}), bf16[16,1,80,1536]{3,2,1,0:T(8,128)(2,1)}, u32[]{:S(2)}, u32[]{:S(2)}) async-start(bf16[16,1,80,1536]{3,2,1,0:T(8,128)(2,1)} %fusion.15), calls=%async_computation.3 | async-start | bytes 7864320 | tf_op jit(solution)/shard_map/all_to_all | solution.py:232
  521.3 447.2 %all-reduce.6.cloned.1.call-start = ((), (), s32[]{:S(2)}) async-start(), calls=%async_computation.18 | async-start | bytes 25276416
  666.2 331.4 %reduce-scatter.8.cloned.1.call-start = ((), (), s32[]{:S(2)}) async-start(), calls=%async_computation.17 | async-start | bytes 2359296 | tf_op jit(solution)/shard_map/reduce_scatter | solution.py:327
  673.0 353.5 %reduce-scatter.6.cloned.1.call-start = ((), (), s32[]{:S(2)}) async-start(), calls=%async_computation.16 | async-start | bytes 2359296 | tf_op jit(solution)/shard_map/reduce_scatter | solution.py:324
  679.4 376.1 %reduce-scatter.4.cloned.1.call-start = ((), (), s32[]{:S(2)}) async-start(), calls=%async_computation.15 | async-start | bytes 2359296 | tf_op jit(solution)/shard_map/reduce_scatter | solution.py:321
  685.5 609.3 %all-reduce.4.cloned.1.call-start = ((), (), s32[]{:S(2)}) async-start(), calls=%async_computation.14 | async-start | bytes 25276416 | tf_op jit(solution)/shard_map/psum | solution.py:300
  1000.1 57.8 %copy-start.49 = (f32[128]{0:T(128)S(1)}, f32[128]{0:T(128)}, u32[]{:S(2)}) copy-start(f32[128]{0:T(128)} %get-tuple-element.69) | copy-start | bytes 1540
  1000.1 57.9 %copy-start.9 = (f32[128,1536]{1,0:T(8,128)S(1)}, f32[128,1536]{1,0:T(8,128)}, u32[]{:S(2)}) copy-start(f32[128,1536]{1,0:T(8,128)} %get-tuple-element.96) | copy-start | bytes 2359300
  (45 other events, 170.5 us)
Sparse Core Ops, SparseCore 0:
  10.1 30.0 all-gather.9
  42.3 27.2 all-gather.11
  71.7 62.6 all-gather.13
  136.4 62.6 all-gather.15
  214.0 27.5 all-gather.19
  243.5 27.1 all-gather.17
  272.9 27.2 all-gather.21
  666.3 302.1 all-reduce.5
  971.3 26.2 reduce-scatter.7
  1000.4 26.0 reduce-scatter.5
  1029.3 26.0 reduce-scatter.3
  1059.6 235.1 all-reduce.3
where the time goes:
time: 1420 us; the launch traced here: 1410 us
  waiting for transfers between devices  919 us (65%)
  local copies, waits for them, and re-layouts  173 us (12%)
  blocking collectives  120 us (8%)
  matrix products  94.9 us (7%)
  other arithmetic  57.7 us (4%)
  starting transfers between devices  29.4 us (2%)
  between operations  15.5 us (1%)
    unnamed x13, waiting for transfers between devices  283 us
    psum x1, waiting for transfers between devices, shards(): lax.psum(lax.psum_scatter(packed.astype(jnp.bfloat16), 'dp', scatter_dime...  236 us
    all_to_all x1, blocking collectives, shards(): lax.all_to_all(result_grad, 'expert', split_axis=0, concat_axis=0, tiled=...  106 us
    slice x4, local copies, waits for them, and re-layouts, shards(): pieces_out.append(flat_sum[offset:offset + amount].reshape(shard_shape))  72.6 us
    all_to_all x1, waiting for transfers between devices, shards(): lax.all_to_all(row_grad, 'expert', split_axis=0, concat_axis=0, tiled=True)  64.8 us
    all_gather x1, waiting for transfers between devices, shards(): lax.all_gather(narrow(w_query), 'dp', axis=0, tiled=True)  61.9 us
    all_gather x1, waiting for transfers between devices, shards(): lax.all_gather(narrow(w_out), 'dp', axis=0, tiled=True)  58.7 us
    all_to_all x1, waiting for transfers between devices, shards(): lax.all_to_all(result, 'expert', split_axis=0, concat_axis=0, tiled=True)  58.3 us
  transfers between devices with their start and end apart: 15, of which 14 were waited for; matrix products, arithmetic and copies ran while one was open for 8% of the time, Pallas kernels for 0%

commit v1 on v0

v1 whole, which is shorter than its diff:
```python
import jax
import jax.numpy as jnp
import numpy as np
from jax import lax
from jax.experimental import pallas as pl
from jax.experimental.pallas import tpu as pltpu
from jax.sharding import PartitionSpec as P

HEAD = 64
norm_eps = 1e-06
score_scale = 0.015625
rope_base = 10000.0
mask_fill = -1e30
BF = jnp.bfloat16
F32 = jnp.float32


def narrow(v):
    return v.astype(BF)


def wide(v):
    return v.astype(F32)


def mm(a, b):
    return jnp.dot(a, b, preferred_element_type=F32)


def mm_tn(a, b):
    return lax.dot_general(a, b, (((0,), (0,)), ((), ())), preferred_element_type=F32)


def mm_nt(a, b):
    return lax.dot_general(a, b, (((1,), (1,)), ((), ())), preferred_element_type=F32)


def add_low(a, b):
    return narrow(wide(a) + wide(b))


def rotary(v, places, heads, sign):
    half = HEAD // 2
    inverse = rope_base ** (-jnp.arange(half, dtype=F32) * 2.0 / HEAD)
    angles = places.astype(F32)[:, None] * inverse[None, :]
    cosine = jnp.cos(angles)[:, None, :]
    sine = sign * jnp.sin(angles)[:, None, :]
    s = v.reshape(v.shape[0], heads, HEAD)
    a, b = s[..., :half], s[..., half:]
    return jnp.concatenate([a * cosine - b * sine, b * cosine + a * sine], -1).reshape(v.shape)


def layout(lengths, length):
    pieces = lengths.shape[0]
    order = jnp.arange(pieces, dtype=jnp.int32)
    ends = jnp.sum(jnp.where(order[None, :] <= order[:, None], lengths[None, :], 0), 1)
    starts = ends - lengths
    at = jnp.arange(length, dtype=jnp.int32)
    segment = jnp.sum((at[:, None] >= ends[None, :]).astype(jnp.int32), 1)
    owned = segment[:, None] == order[None, :]
    places = at - jnp.sum(jnp.where(owned, starts[None, :], 0), 1)
    live = segment < pieces - 1
    allowed = (
        (segment[:, None] == segment[None, :])
        & (at[None, :] <= at[:, None])
        & (live[None, :] | (at[:, None] == at[None, :]))
    )
    return places, live, allowed


def put_rows(pair, at, widths):
    rows, per = pair[0].shape[0] * 2, pair[0].shape[0] * 2 // at.shape[0]
    c = at.shape[0] // 2
    total = sum(widths)
    cuts = [sum(widths[:i]) for i in range(len(widths) + 1)]
    if per % 16:
        out = jnp.zeros((rows, total), F32)
        for i in range(2 * c):
            blk = wide(pair[i // c][i % c * per : (i % c + 1) * per])
            out = lax.dynamic_update_slice_in_dim(out, blk, at[i] * per, 0)
        return [out[:, a:b] for a, b in zip(cuts, cuts[1:])]

    def body(at_ref, own, sib, *outs):
        def write(src):
            for ref, a, b in zip(outs, cuts, cuts[1:]):
                ref[...] = wide(src[:, a:b])

        @pl.when(pl.program_id(0) < c)
        def _():
            write(own)

        @pl.when(pl.program_id(0) >= c)
        def _():
            write(sib)

    return pl.pallas_call(
        body,
        grid_spec=pltpu.PrefetchScalarGridSpec(
            num_scalar_prefetch=1,
            grid=(2 * c,),
            in_specs=[
                pl.BlockSpec((per, total), lambda i, at: (jnp.minimum(i, c - 1), 0)),
                pl.BlockSpec((per, total), lambda i, at: (jnp.maximum(i - c, 0), 0)),
            ],
            out_specs=[pl.BlockSpec((per, w), lambda i, at: (at[i], 0)) for w in widths],
        ),
        out_shape=[jax.ShapeDtypeStruct((rows, w), F32) for w in widths],
        cost_estimate=pl.CostEstimate(
            flops=rows * total, bytes_accessed=rows * total * 6, transcendentals=0
        ),
        name="put_rows",
    )(at, *pair)


def expert_step(spots, rows, cots, weights, kept, start, total):
    gate_w, up_w, down_w, router = weights
    n, width = rows[0].shape
    ffe = gate_w.shape[1]
    tail = router.shape[0]
    block = cots.shape[0] // spots[1]
    steps = n // block
    two = 2 * block

    def body(spot, xa, xb, ca, cb, gw, uw, dw, rt, *refs):
        mix_a, mix_b, row_a, row_b, x_o, hid_o, gpg_o, upg_o, rg_o = refs[-9:]
        x = jnp.concatenate([xa[...], xb[...]])
        cm = jnp.concatenate([ca[...], cb[...]])
        cot, chosen = wide(cm[:, :width]), cm[:, width:] > 0
        x_o[...] = x
        logits = jnp.where(chosen, mm_nt(x, rt[...]), mask_fill)
        top = jnp.max(logits, -1, keepdims=True)
        raised = jnp.where(chosen, jnp.exp(logits - top), 0.0)
        mine = lax.broadcasted_iota(jnp.int32, raised.shape, 1)
        gate = jnp.sum(jnp.where(mine == spot[0], raised, 0.0), -1, keepdims=True)
        gate = wide(narrow(gate / jnp.sum(raised, -1, keepdims=True)))
        gate_pre, up_pre = mm(x, gw[...]), mm(x, uw[...])
        sg = jax.nn.sigmoid(gate_pre)
        silu = gate_pre * sg
        hidden = narrow(silu * up_pre)
        hid_o[...] = hidden
        result_grad = narrow(gate * cot)
        rg_o[...] = result_grad
        result = wide(narrow(mm(hidden, dw[...])))
        mix = narrow(gate * result)
        mix_a[...], mix_b[...] = mix[:block], mix[block:]
        gate_grad = jnp.sum(result * cot, -1, keepdims=True)
        hidden_grad = mm_nt(result_grad, dw[...])
        gpg = narrow(hidden_grad * up_pre * sg * (1.0 + gate_pre * (1.0 - sg)))
        upg = narrow(hidden_grad * silu)
        gpg_o[...], upg_o[...] = gpg, upg
        row = narrow(mm_nt(gpg, gw[...]) + mm_nt(upg, uw[...]))
        row_a[:, :width], row_b[:, :width] = row[:block], row[block:]
        high = wide(narrow(gate_grad))
        ends = jnp.where(mine == spot[0], high, 0.0)
        ends = narrow(jnp.where(mine == spot[0] + tail // 2, gate_grad - high, ends))
        row_a[:, width:], row_b[:, width:] = ends[:block], ends[block:]

    whole = lambda a: pl.BlockSpec(a.shape, lambda i, s: (0, 0))
    step = lambda w: pl.BlockSpec((block, w), lambda i, s: (i, 0))
    keep = lambda w: pl.BlockSpec((two, w), lambda i, s: (start + i, 0))
    widths = [width, ffe, ffe, ffe, width]
    out_shape = [jax.ShapeDtypeStruct((n, w), BF) for w in (width, width, width + tail, width + tail)]
    out_shape += [jax.ShapeDtypeStruct((total, w), BF) for w in widths]
    given = list(kept or ())
    return pl.pallas_call(
        body,
        grid_spec=pltpu.PrefetchScalarGridSpec(
            num_scalar_prefetch=1,
            grid=(steps,),
            in_specs=[
                step(width),
                step(width),
                pl.BlockSpec((block, width + tail), lambda i, s: (s[1 + i], 0)),
                pl.BlockSpec((block, width + tail), lambda i, s: (s[1 + steps + i], 0)),
                whole(gate_w),
                whole(up_w),
                whole(down_w),
                whole(router),
            ]
            + [pl.BlockSpec(memory_space=pl.ANY)] * len(given),
            out_specs=[step(width), step(width), step(width + tail), step(width + tail)]
            + [keep(w) for w in widths],
        ),
        out_shape=out_shape,
        input_output_aliases={9 + i: 4 + i for i in range(len(given))},
        compiler_params=pltpu.CompilerParams(vmem_limit_bytes=48 << 20),
        cost_estimate=pl.CostEstimate(
            flops=12 * 2 * n * width * ffe,
            bytes_accessed=6 * width * ffe + 2 * n * width * 16,
            transcendentals=2 * n * ffe,
        ),
        name="expert_step",
    )(jnp.asarray(spots[0]), *rows, cots, cots, *weights, *given)


class Links:
    def __init__(self):
        self.n = lax.axis_size("dp")
        self.e = lax.axis_size("expert")
        self.chips = self.e // 2
        order = list(range(self.chips))
        if self.n == 2 and self.chips == 8:
            order = [0, 2, 4, 6, 7, 5, 3, 1]
        self.order = order
        where = np.argsort(np.array(order)).astype(np.int32)
        self.x = lax.axis_index("dp")
        self.me = lax.axis_index("expert")
        self.core = self.me % 2
        chip = self.me // 2
        self.place = jnp.sum(
            jnp.where(jnp.arange(self.chips, dtype=jnp.int32) == chip, jnp.asarray(where), 0)
        )

    def at(self, r, lane):
        place = (self.place + r) % self.chips
        order = jnp.asarray(np.array(self.order, np.int32))
        chip = jnp.sum(jnp.where(jnp.arange(self.chips, dtype=jnp.int32) == place, order, 0))
        return chip * 2 + (self.core ^ lane)

    def sibling(self, v):
        return lax.ppermute(v, "expert", [(i, i ^ 1) for i in range(self.e)])

    def flip(self, v, bit):
        return lax.ppermute(v, "expert", [(i, i ^ bit) for i in range(self.e)])

    def ring(self, v, step):
        c, o = self.chips, self.order
        pairs = [(o[k] * 2 + l, o[(k + step) % c] * 2 + l) for k in range(c) for l in (0, 1)]
        return lax.ppermute(v, "expert", pairs)

    def gather(self, block):
        c = self.chips
        half = block.shape[0] // 2
        got = {0: block}
        up = down = block
        for s in range(1, c // 2):
            up, down = self.ring(up, 1), self.ring(down, -1)
            got[c - s], got[s] = up, down
        far = (self.ring(up[:half], 1), self.ring(down[half:], -1))
        return got, far

    def scatter(self, s, far):
        c = self.chips
        half = far[0].shape[0]
        up, down = self.ring(far[0], 1), self.ring(far[1], -1)
        r = c // 2 - 1
        up = jnp.concatenate([add_low(up, s[r][:half]), s[r][half:]])
        down = jnp.concatenate([s[c - r][:half], add_low(down, s[c - r][half:])])
        up, down = self.ring(up, 1), self.ring(down, -1)
        for r in range(c // 2 - 2, 0, -1):
            up, down = self.ring(add_low(up, s[r]), 1), self.ring(add_low(down, s[c - r]), -1)
        return wide(s[0]) + wide(up) + wide(down)

    def swap(self, v):
        return lax.ppermute(v, "dp", [(0, 1), (1, 0)])

    def pick(self, v, other, axis):
        size = v.shape[axis] // self.n
        at = (1 - self.x if other else self.x) * size
        return lax.dynamic_slice_in_dim(v, at, size, axis)

    def both(self, own, got, axis):
        return jnp.where(
            self.x == 0,
            jnp.concatenate([own, got], axis),
            jnp.concatenate([got, own], axis),
        )

    def columns(self, v):
        if self.n == 2:
            return jnp.concatenate([self.pick(v, False, 1), self.swap(self.pick(v, True, 1))])
        return lax.all_to_all(v, "dp", split_axis=1, concat_axis=0, tiled=True)

    def columns_back(self, v):
        if self.n == 2:
            t = v.shape[0] // 2
            return self.both(v[:t], wide(self.swap(narrow(v[t:]))), 1)
        return wide(lax.all_to_all(narrow(v), "dp", split_axis=0, concat_axis=1, tiled=True))

    def rows(self, v):
        if self.n == 2:
            return jnp.concatenate([v, self.swap(v)])
        return lax.all_gather(v, "dp", axis=0, tiled=True)

    def sum_back(self, v):
        if self.n == 2:
            t = v.shape[0] // 2
            return v[:t] + wide(self.swap(narrow(v[t:])))
        return wide(lax.psum_scatter(narrow(v), "dp", scatter_dimension=0, tiled=True))

    def whole(self, v, axis):
        if self.n == 2:
            return self.both(v, self.swap(v), axis)
        return lax.all_gather(v, "dp", axis=axis, tiled=True)

    def shard_sum(self, v, axis):
        if self.n == 2:
            return self.pick(v, False, axis) + wide(self.swap(narrow(self.pick(v, True, axis))))
        return wide(lax.psum_scatter(narrow(v), "dp", scatter_dimension=axis, tiled=True))

    def whole_out(self, w):
        if self.n != 2 or self.e % 4:
            return lax.all_gather(w, "dp", axis=0, tiled=True)
        rows = w.shape[0]
        part = rows // 4
        q = self.me % 4
        a = self.swap(lax.dynamic_slice_in_dim(w, q * part, part, 0))
        b = self.flip(a, 2)
        c, d = self.flip(a, 1), self.flip(b, 1)
        full = jnp.zeros((rows * 2, w.shape[1]), w.dtype)
        full = lax.dynamic_update_slice_in_dim(full, w, self.x * rows, 0)
        for piece, at in ((a, q), (b, q ^ 2), (c, q ^ 1), (d, q ^ 3)):
            full = lax.dynamic_update_slice_in_dim(full, piece, (1 - self.x) * rows + at * part, 0)
        return full


def shards(
    tokens, cotangent, lengths, routes, gain_attn, w_query, key_weight, value_weight,
    w_out, gain_moe, w_router, w_gate, w_up, w_down,
):
    net = Links()
    c = net.chips
    length, width = tokens.shape
    dh = gain_attn.shape[0]
    heads = w_query.shape[1] // HEAD
    kv_heads = key_weight.shape[1] // HEAD
    group = heads // kv_heads
    fq, fk = w_query.shape[1], key_weight.shape[1]
    experts = w_router.shape[1]
    places, live, allowed = layout(lengths[0], length)

    stream = wide(tokens)
    inv_one = lax.rsqrt(jnp.mean(stream * stream, -1, keepdims=True) + norm_eps)
    token_cols = wide(net.columns(tokens))
    inv_all = net.rows(inv_one.reshape(1, length)).reshape(-1, 1)
    scaled_cols = token_cols * inv_all
    gain_one_low = wide(narrow(gain_attn))[None, :]
    normed_cols = narrow(scaled_cols * gain_one_low)
    w_qkv = jnp.concatenate([narrow(w_query), narrow(key_weight), narrow(value_weight)], 1)
    qkv = net.sum_back(mm(normed_cols, w_qkv))

    small = jnp.concatenate(
        [narrow(w_router).T, narrow(gain_attn)[None], narrow(gain_moe)[None]], 0
    )
    small = net.whole(small, 1)
    router_t, gain_one, gain_two = small[:experts], wide(small[experts]), wide(small[experts + 1])
    out_full = net.whole_out(narrow(w_out))
    mask = jnp.sum(
        (routes[:, :, None] == jnp.arange(experts, dtype=jnp.int32)[None, None, :]).astype(F32), 1
    )
    tail = 128
    cot_mask = jnp.concatenate(
        [cotangent, narrow(jnp.pad(mask, ((0, 0), (0, tail - experts))))], 1
    )
    cot_all = lax.all_gather(cot_mask, "expert", axis=0, tiled=True)
    router_pad = jnp.pad(router_t, ((0, tail - experts), (0, 0)))

    qkv_d, wg, wu, wd = lax.optimization_barrier(
        (qkv, narrow(w_gate[0]), narrow(w_up[0]), narrow(w_down[0]))
    )
    qkv = qkv_d
    gate_full, up_full = net.whole(wg, 0), net.whole(wu, 0)
    down_full = net.whole(wd, 0)

    q = narrow(rotary(qkv[:, :fq], places, heads, 1.0)).reshape(length, kv_heads, group, HEAD)
    k = narrow(rotary(qkv[:, fq : fq + fk], places, kv_heads, 1.0)).reshape(length, kv_heads, HEAD)
    v = narrow(qkv[:, fq + fk :]).reshape(length, kv_heads, HEAD)
    scores = score_scale * jnp.einsum("sngh,tnh->ngst", q, k, preferred_element_type=F32)
    masked = jnp.where(allowed, scores, mask_fill)
    peak = jnp.max(masked, -1, keepdims=True)
    raised = jnp.exp(masked - peak)
    attention = raised / jnp.sum(raised, -1, keepdims=True)
    attention_low = narrow(attention)
    context = jnp.einsum("ngst,tnh->sngh", attention_low, v, preferred_element_type=F32)
    context = context.reshape(length, fq)
    attended = narrow(jnp.where(live[:, None], context, 0.0))
    stream_mid = stream + mm(attended, out_full)
    inv_two = lax.rsqrt(jnp.mean(stream_mid * stream_mid, -1, keepdims=True) + norm_eps)
    scaled_two = stream_mid * inv_two
    normed_two = narrow(scaled_two * gain_two)

    def gates(rows, chosen):
        logits = jnp.where(chosen > 0, mm_nt(rows, router_t), mask_fill)
        top = jnp.max(logits, -1, keepdims=True)
        up = jnp.where(chosen > 0, jnp.exp(logits - top), 0.0)
        return up / jnp.sum(up, -1, keepdims=True)

    gate_own = gates(normed_two, mask)

    rows_got, rows_far = net.gather(normed_two)
    half = length // 2
    groups = [[0]] + [[s, c - s] for s in range(1, c // 2)] + [[c // 2]]
    kept, start, mixes, backs = None, 0, {}, {}
    weights = (gate_full, up_full, down_full, router_pad)
    for g in groups:
        if g == [c // 2]:
            x0 = jnp.concatenate(rows_far)
        else:
            x0 = jnp.concatenate([rows_got[r] for r in g])
        spots = [net.me] + [net.at(r, l) for l in (0, 1) for r in g]
        spots = (jnp.stack(spots).astype(jnp.int32), net.e)
        out = expert_step(
            spots, (x0, net.sibling(x0)), cot_all, weights, kept, start, net.e * length
        )
        kept, start = out[4:], start + len(g)
        for store, a, b in ((mixes, out[0], out[1]), (backs, out[2], out[3])):
            s = add_low(a, net.sibling(b))
            for i, r in enumerate(g):
                store[r] = s[i * length : (i + 1) * length]
    far = c // 2
    back = net.scatter(backs, (backs[far][:half], backs[far][half:]))
    mixed = narrow(stream_mid + net.scatter(mixes, (mixes[far][:half], mixes[far][half:])))

    rows_all, hid_all, gpg_all, upg_all, rg_all = kept
    d_down = net.shard_sum(mm_tn(hid_all, rg_all), 0)[None]
    d_gate = net.shard_sum(mm_tn(rows_all, gpg_all), 0)[None]
    d_up = net.shard_sum(mm_tn(rows_all, upg_all), 0)[None]

    ends = back[:, width:]
    gate_grad = ends[:, :experts] + ends[:, tail // 2 : tail // 2 + experts]
    chosen = gate_own * (gate_grad - jnp.sum(gate_own * gate_grad, -1, keepdims=True))
    logit_grad = narrow(chosen)
    n2g = back[:, :width] + mm(logit_grad, router_t)
    du = n2g * gain_two
    mid_grad = wide(cotangent) + inv_two * (
        du - scaled_two * jnp.mean(du * scaled_two, -1, keepdims=True)
    )
    d_small = jnp.concatenate(
        [mm_tn(logit_grad, normed_two), jnp.sum(n2g * scaled_two, 0)[None]], 0
    )
    d_small = net.shard_sum(d_small, 1)
    branch = narrow(mid_grad)

    per = dh // net.e
    slot = jnp.arange(dh, dtype=jnp.int32)
    lane, dist, inner = slot // (c * per), (slot // per) % c, slot % per
    source = (((net.place + dist) % c) * 2 + (net.core ^ lane)) * per + inner
    perm = (slot[:, None] == source[None, :]).astype(BF)

    seats = jnp.stack(
        [((net.place + r) % c) * 2 + (net.core ^ l) for l in (0, 1) for r in range(c)]
    ).astype(jnp.int32)

    def all_sum(d, widths):
        n = c * per
        s = add_low(d[:n], net.sibling(d[n:]))
        s = {r: s[r * per : (r + 1) * per] for r in range(c)}
        far = c // 2
        cut = per // 2
        total = net.scatter(s, (s[far][:cut], s[far][cut:]))
        got, ends = net.gather(narrow(total))
        got[far] = jnp.concatenate(ends)
        own = jnp.concatenate([got[r] for r in range(c)])
        return put_rows((own, net.sibling(own)), seats, widths)

    attended_cols = narrow(mm(net.columns(attended), perm))
    branch_all = net.rows(branch)
    [d_out] = all_sum(narrow(mm_tn(attended_cols, branch_all)), [width])

    zero = jnp.zeros((), BF)
    cg = jnp.where(live[:, None], narrow(mm_nt(branch, out_full)), zero)
    cg = cg.reshape(length, kv_heads, group, HEAD)
    ag = jnp.einsum("sngh,tnh->ngst", cg, v, preferred_element_type=F32)
    vg = narrow(jnp.einsum("ngst,sngh->tnh", attention_low, cg, preferred_element_type=F32))
    sgr = narrow(attention * (ag - jnp.sum(attention * ag, -1, keepdims=True)))
    qg = score_scale * jnp.einsum("ngst,tnh->sngh", sgr, k, preferred_element_type=F32)
    kg = score_scale * jnp.einsum("ngst,sngh->tnh", sgr, q, preferred_element_type=F32)
    qpg = narrow(rotary(qg.reshape(length, fq), places, heads, -1.0))
    kpg = narrow(rotary(kg.reshape(length, fk), places, kv_heads, -1.0))
    grads = jnp.concatenate([qpg, kpg, vg.reshape(length, fk)], 1)
    grads_all = net.rows(grads)
    normed_ring = narrow(mm(normed_cols, perm))
    d_qkv = mm_tn(normed_ring, grads_all)
    n1g_cols = mm_nt(grads_all, w_qkv)
    d_gain_one = jnp.sum(n1g_cols * scaled_cols, 0)[None]
    d_small = mm(narrow(jnp.concatenate([d_small, d_gain_one], 0)), perm)
    d_small = jnp.pad(d_small.T, ((0, 0), (0, 128 - experts - 2)))
    d_query, d_key, d_value, d_small = all_sum(
        narrow(jnp.concatenate([d_qkv, d_small], 1)), [fq, fk, fk, 128]
    )
    n1g = net.columns_back(n1g_cols)
    scaled_one = stream * inv_one
    du = n1g * gain_one
    d_tokens = mid_grad + inv_one * (
        du - scaled_one * jnp.mean(du * scaled_one, -1, keepdims=True)
    )
    return (
        mixed,
        d_tokens,
        d_small[:, experts + 1],
        d_query,
        d_key,
        d_value,
        d_out,
        d_small[:, experts],
        d_small[:, :experts],
        d_gate,
        d_up,
        d_down,
    )


def solution(mesh):
    rows = P(("dp", "expert"), None)
    flat, dense, routed = P("dp"), P("dp", None), P("expert", "dp", None)
    return jax.shard_map(
        shards,
        mesh=mesh,
        in_specs=(
            rows, rows, rows, rows, flat, dense, dense, dense, dense, flat, dense,
            routed, routed, routed,
        ),
        out_specs=(
            rows, rows, flat, dense, dense, dense, dense, flat, dense, routed, routed, routed,
        ),
        check_vma=False,
    )
```

time: 1420 us -> 545 us (0.38)
  waiting for transfers between devices: 919 us -> 204 us
  blocking collectives: 120 us -> 0 us
  local copies, waits for them, and re-layouts: 173 us -> 54.6 us
  Pallas kernels: 0 us -> 70.7 us
  matrix products: 94.9 us -> 45.9 us
  starting transfers between devices: 29.4 us -> 76.3 us
    unnamed x13 -> x1, waiting for transfers between devices: 283 us -> 0.02 us
    psum x1 -> x0, waiting for transfers between devices: 236 us -> none  [shards(): lax.psum(lax.psum_scatter(packed.astype(jnp.bfloat16), 'dp', scatter_dime...]
    ppermute x0 -> x94, waiting for transfers between devices: none -> 204 us  [the longest x56 143 us: ring(): return lax.ppermute(v, 'expert', pairs)]
    all_gather x7 -> x1, waiting for transfers between devices: 173 us -> 0.01 us  [shards(): cot_all = lax.all_gather(cot_mask, 'expert', axis=0, tiled=True)]
    all_to_all x3 -> x0, waiting for transfers between devices: 166 us -> none  [the longest x1 64.8 us: shards(): lax.all_to_all(row_grad, 'expert', split_axis=0, concat_axis=0, tiled=True)]
    all_to_all x1 -> x0, blocking collectives: 106 us -> none  [shards(): lax.all_to_all(result_grad, 'expert', split_axis=0, concat_axis=0, tiled=...]
    ppermute x0 -> x94, starting transfers between devices: none -> 76.2 us  [the longest x56 53.1 us: ring(): return lax.ppermute(v, 'expert', pairs)]
    pallas_call x0 -> x7, Pallas kernels: none -> 70.7 us  [the longest x5 48 us: expert_step(): pl.pallas_call(body, grid_spec=pltpu.PrefetchScalarGridSpec(num_scalar_pr...]
  transfers between devices with their start and end apart: 15 -> 95, of which waited for: 14 -> 44; matrix products, arithmetic and copies ran while one was open for 8% -> 26% of each run, Pallas kernels for 0% -> 11%
where the time goes in v1:
time: 545 us; the launch traced here: 535 us
  waiting for transfers between devices  204 us (37%)
  starting transfers between devices  76.3 us (14%)
  Pallas kernels  70.7 us (13%)
  other arithmetic  55.5 us (10%)
  local copies, waits for them, and re-layouts  54.6 us (10%)
  matrix products  45.9 us (8%)
  between operations  27.8 us (5%)
    ppermute x56, waiting for transfers between devices, ring(): return lax.ppermute(v, 'expert', pairs)  143 us
    ppermute x16, waiting for transfers between devices, swap(): return lax.ppermute(v, 'dp', [(0, 1), (1, 0)])  60.7 us
    ppermute x56, starting transfers between devices, ring(): return lax.ppermute(v, 'expert', pairs)  53.1 us
    pallas_call x5, Pallas kernels, expert_step(): pl.pallas_call(body, grid_spec=pltpu.PrefetchScalarGridSpec(num_scalar_pr...  48 us
    unnamed x225, local copies, waits for them, and re-layouts  23.7 us
    dot_general x6, matrix products, mm_tn(): lax.dot_general(a, b, (((0,), (0,)), ((), ())), preferred_element_type=F32)  23.7 us
    pallas_call x2, Pallas kernels, put_rows(): pl.pallas_call(body, grid_spec=pltpu.PrefetchScalarGridSpec(num_scalar_pr...  22.7 us
    ppermute x16, starting transfers between devices, swap(): return lax.ppermute(v, 'dp', [(0, 1), (1, 0)])  19.2 us
  transfers between devices with their start and end apart: 95, of which 44 were waited for; matrix products, arithmetic and copies ran while one was open for 26% of the time, Pallas kernels for 11%

profile of v1, /device:TPU:0, one launch (start us, length us, event | category | flops | bytes accessed | tf_op | source)
XLA Modules:
  0.0 534.6 jit_solution(2800219067328272903)
XLA Ops:
  84.0 6.5 %collective-permute-done.9 = bf16[768,512]{1,0:T(8,128)(2,1)} collective-permute-done((bf16[768,512]{1,0:T(8,128)(2,1)S(1)}, bf16[768,512]{1,0:T(8,128)(2,1)}, u32[]{:S(2)}, u32[]{:S(2)}) %collective-permute-start.9) | collective-permute-done | bytes 786464 | tf_op jit(solution)/shard_map/ppermute | solution.py:255
  92.4 14.9 %collective-permute-done.10 = bf16[768,512]{1,0:T(8,128)(2,1)} collective-permute-done((bf16[768,512]{1,0:T(8,128)(2,1)S(1)}, bf16[768,512]{1,0:T(8,128)(2,1)}, u32[]{:S(2)}, u32[]{:S(2)}) %collective-permute-start.10) | collective-permute-done | bytes 786464 | tf_op jit(solution)/shard_map/ppermute | solution.py:255
  116.5 7.7 %collective-permute-done.11 = bf16[256,1536]{1,0:T(8,128)(2,1)} collective-permute-done((bf16[256,1536]{1,0:T(8,128)(2,1)}, bf16[256,1536]{1,0:T(8,128)(2,1)}, u32[]{:S(2)}, u32[]{:S(2)}) %collective-permute-start.11) | collective-permute-done | bytes 786464 | tf_op jit(solution)/shard_map/ppermute | solution.py:255
  131.8 7.9 %collective-permute-done.18 = bf16[128,1536]{1,0:T(8,128)(2,1)S(1)} collective-permute-done((bf16[128,1536]{1,0:T(8,128)(2,1)S(1)}, bf16[128,1536]{1,0:T(8,128)(2,1)S(1)}, u32[]{:S(2)}, u32[]{:S(2)}) %collective-permute-start.18) | collective-permute-done | bytes 393248 | tf_op jit(solution)/shard_map/ppermute | solution.py:229
  143.4 7.3 %collective-permute-done.15 = bf16[128,1536]{1,0:T(8,128)(2,1)S(1)} collective-permute-done((bf16[128,1536]{1,0:T(8,128)(2,1)S(1)}, bf16[128,1536]{1,0:T(8,128)(2,1)S(1)}, u32[]{:S(2)}, u32[]{:S(2)}) %collective-permute-start.15) | collective-permute-done | bytes 393248 | tf_op jit(solution)/shard_map/ppermute | solution.py:229
  160.7 4.3 collective-permute-done.20
  169.0 6.3 %expert_step.5 = (bf16[128,1536]{1,0:T(8,128)(2,1)S(1)}, bf16[128,1536]{1,0:T(8,128)(2,1)S(1)}, bf16[128,1664]{1,0:T(8,128)(2,1)S(1)}, bf16[128,1664]{1,0:T(8,12...) custom-call(s32[3]{0:T(128)S(1)} %pad_add_fusion.spot, ...), custom_call_target="tpu_custom_call" | custom-call | flops 2415919104 | bytes 11010048 | tf_op jit(solution)/shard_map/expert_step/pallas_call | solution.py:165
  179.0 11.6 %expert_step.6 = (bf16[256,1536]{1,0:T(8,128)(2,1)S(1)}, bf16[256,1536]{1,0:T(8,128)(2,1)}, bf16[256,1664]{1,0:T(8,128)(2,1)S(1)}, bf16[256,1664]{1,0:T(8,128)(2...) custom-call(s32[5]{0:T(128)S(1)} %copy-done.13, ...), custom_call_target="tpu_custom_call", output_to_operand_aliasing={{4}: (9, {}), {5}: (10, {}), {6}: (11, {}), {7}: (12, {}), ... | custom-call | flops 4831838208 | bytes 17301504 | tf_op jit(solution)/shard_map/expert_step/pallas_call | solution.py:165
  190.7 11.6 %expert_step.7 = (bf16[256,1536]{1,0:T(8,128)(2,1)S(1)}, bf16[256,1536]{1,0:T(8,128)(2,1)}, bf16[256,1664]{1,0:T(8,128)(2,1)S(1)}, bf16[256,1664]{1,0:T(8,128)(2...) custom-call(s32[5]{0:T(128)S(1)} %stack.137.spot, ...), custom_call_target="tpu_custom_call", output_to_operand_aliasing={{4}: (9, {}), {5}: (10, {}), {6}: (11, {}), {7}: (12, {}), ... | custom-call | flops 4831838208 | bytes 17301504 | tf_op jit(solution)/shard_map/expert_step/pallas_call | solution.py:165
  202.8 11.6 %expert_step.8 = (bf16[256,1536]{1,0:T(8,128)(2,1)S(1)}, bf16[256,1536]{1,0:T(8,128)(2,1)S(1)}, bf16[256,1664]{1,0:T(8,128)(2,1)S(1)}, bf16[256,1664]{1,0:T(8,12...) custom-call(s32[5]{0:T(128)S(1)} %stack.132.spot, ...), custom_call_target="tpu_custom_call", output_to_operand_aliasing={{4}: (9, {}), {5}: (10, {}), {6}: (11, {}), {7}: (12, {}), ... | custom-call | flops 4831838208 | bytes 17301504 | tf_op jit(solution)/shard_map/expert_step/pallas_call | solution.py:165
  214.5 6.8 %expert_step.9 = (bf16[128,1536]{1,0:T(8,128)(2,1)S(1)}, bf16[128,1536]{1,0:T(8,128)(2,1)S(1)}, bf16[128,1664]{1,0:T(8,128)(2,1)S(1)}, bf16[128,1664]{1,0:T(8,12...) custom-call(s32[3]{0:T(128)S(1)} %pad_add_fusion.1.spot, ...), custom_call_target="tpu_custom_call", output_to_operand_aliasing={{4}: (9, {}), {5}: (10, {}), {6}: (11, {}), {7}: (12, {}), ... | custom-call | flops 2415919104 | bytes 11010048 | tf_op jit(solution)/shard_map/expert_step/pallas_call | solution.py:165
  221.8 6.5 %fusion.119 = f32[1536,512]{1,0:T(8,128)S(1)} fusion(bf16[2048,1536]{1,0:T(8,128)(2,1)} %get-tuple-element.113, bf16[2048,512]{1,0:T(8,128)(2,1)} %get-tuple-element.114), kind=kOutput, calls=%fused_computation.316 | convolution fusion | flops 3221225472 | bytes 11534336 | tf_op jit(solution)/shard_map/dot_general | solution.py:31
  249.4 8.0 %collective-permute-done.91 = bf16[768,512]{1,0:T(8,128)(2,1)S(1)} collective-permute-done((bf16[768,512]{1,0:T(8,128)(2,1)S(1)}, bf16[768,512]{1,0:T(8,128)(2,1)S(1)}, u32[]{:S(2)}, u32[]{:S(2)}) %collective-permute-start.91) | collective-permute-done | bytes 786464 | tf_op jit(solution)/shard_map/ppermute | solution.py:255
  258.8 15.0 %collective-permute-done.93 = bf16[256,1536]{1,0:T(8,128)(2,1)S(1)} collective-permute-done((bf16[256,1536]{1,0:T(8,128)(2,1)S(1)}, bf16[256,1536]{1,0:T(8,128)(2,1)S(1)}, u32[]{:S(2)}, u32[]{:S(2)}) %collective-permute-start.93) | collective-permute-done | bytes 786464 | tf_op jit(solution)/shard_map/ppermute | solution.py:255
  285.8 7.8 %collective-permute-done.47 = bf16[128,1664]{1,0:T(8,128)(2,1)S(1)} collective-permute-done((bf16[128,1664]{1,0:T(8,128)(2,1)S(1)}, bf16[128,1664]{1,0:T(8,128)(2,1)S(1)}, u32[]{:S(2)}, u32[]{:S(2)}) %collective-permute-start.47) | collective-permute-done | bytes 426016 | tf_op jit(solution)/shard_map/ppermute | solution.py:229
  297.4 8.7 %collective-permute-done.43 = bf16[128,1664]{1,0:T(8,128)(2,1)S(1)} collective-permute-done((bf16[128,1664]{1,0:T(8,128)(2,1)S(1)}, bf16[128,1664]{1,0:T(8,128)(2,1)S(1)}, u32[]{:S(2)}, u32[]{:S(2)}) %collective-permute-start.43) | collective-permute-done | bytes 426016 | tf_op jit(solution)/shard_map/ppermute | solution.py:229
  310.8 6.8 %collective-permute-done.45 = bf16[128,1664]{1,0:T(8,128)(2,1)S(1)} collective-permute-done((bf16[128,1664]{1,0:T(8,128)(2,1)S(1)}, bf16[128,1664]{1,0:T(8,128)(2,1)S(1)}, u32[]{:S(2)}, u32[]{:S(2)}) %collective-permute-start.45) | collective-permute-done | bytes 426016 | tf_op jit(solution)/shard_map/ppermute | solution.py:229
  346.6 6.9 %collective-permute-done.50 = bf16[128,2560]{0,1:T(8,128)(2,1)} collective-permute-done((bf16[128,2560]{0,1:T(8,128)(2,1)}, bf16[128,2560]{0,1:T(8,128)(2,1)}, u32[]{:S(2)}, u32[]{:S(2)}) %collective-permute-start.50) | collective-permute-done | bytes 655392 | tf_op jit(solution)/shard_map/ppermute | solution.py:255
  360.0 5.2 convolution_convert_fusion
  386.8 7.8 %collective-permute-done.76 = bf16[48,1536]{1,0:T(8,128)(2,1)S(1)} collective-permute-done((bf16[48,1536]{1,0:T(8,128)(2,1)S(1)}, bf16[48,1536]{1,0:T(8,128)(2,1)S(1)}, u32[]{:S(2)}, u32[]{:S(2)}) %collective-permute-start.76) | collective-permute-done | bytes 147488 | tf_op jit(solution)/shard_map/ppermute | solution.py:229
  396.6 4.2 collective-permute-done.54
  403.0 4.6 collective-permute-done.77
  409.7 6.9 %collective-permute-done.59 = bf16[48,2688]{1,0:T(8,128)(2,1)S(1)} collective-permute-done((bf16[48,2688]{1,0:T(8,128)(2,1)S(1)}, bf16[48,2688]{1,0:T(8,128)(2,1)S(1)}, u32[]{:S(2)}, u32[]{:S(2)}) %collective-permute-start.59) | collective-permute-done | bytes 258080 | tf_op jit(solution)/shard_map/ppermute | solution.py:229
  424.2 6.8 %collective-permute-done.86 = bf16[48,1536]{1,0:T(8,128)(2,1)S(1)} collective-permute-done((bf16[48,1536]{1,0:T(8,128)(2,1)S(1)}, bf16[48,1536]{1,0:T(8,128)(2,1)S(1)}, u32[]{:S(2)}, u32[]{:S(2)}) %collective-permute-start.86) | collective-permute-done | bytes 147488 | tf_op jit(solution)/shard_map/ppermute | solution.py:229
  445.3 4.9 collective-permute-done.88
  454.2 4.6 collective-permute-done.62
  461.6 4.7 collective-permute-done.63
  468.4 4.3 collective-permute-done.64
  478.3 4.3 collective-permute-done.69
  488.8 8.6 %collective-permute-done.32 = bf16[128,1536]{1,0:T(8,128)(2,1)S(1)} collective-permute-done((bf16[128,1536]{1,0:T(8,128)(2,1)S(1)}, bf16[128,1536]{1,0:T(8,128)(2,1)S(1)}, u32[]{:S(2)}, u32[]{:S(2)}) %collective-permute-start.32) | collective-permute-done | bytes 393248 | tf_op jit(solution)/shard_map/ppermute | solution.py:229
  500.5 10.8 %put_rows.3 = f32[768,1536]{1,0:T(8,128)} custom-call(s32[16]{0:T(128)} %stack.159.at_ref, bf16[384,1536]{1,0:T(8,128)(2,1)} %copy-done.46, bf16[384,1536]{1,0:T(8,128)(2,1)} %collective-permute-done.90.sib), custom_call_target="tpu_custom_call" | custom-call | flops 1179648 | bytes 7077888 | tf_op jit(solution)/shard_map/put_rows/pallas_call | solution.py:96
  511.3 12.0 %put_rows.2 = (f32[768,1536]{1,0:T(8,128)}, f32[768,512]{1,0:T(8,128)}, f32[768,512]{1,0:T(8,128)}, f32[768,128]{1,0:T(8,128)}) custom-call(s32[16]{0:T(128)} %stack.159.at_ref, bf16[384,2688]{1,0:T(8,128)(2,1)} %constant_dynamic-update-slice_fusion.8.own, bf16[384,2688]{1,0:T(8,128)(2,1)} %collective-permute-done.70.sib), custom_call_target="tpu_custom_call" | custom-call | flops 2064384 | bytes 12386304 | tf_op jit(solution)/shard_map/put_rows/pallas_call | solution.py:96
  (563 shorter events, 260.9 us)
Async XLA Ops:
  7.2 159.8 %all-gather.2.cloned.1.call-start = ((), (), s32[]{:S(2)}) async-start(), calls=%async_computation | async-start | bytes 7241728 | tf_op jit(solution)/shard_map/all_gather | solution.py:355
  9.0 39.0 %collective-permute-start.1 = (f32[1,128]{1,0:T(1,128)S(1)}, f32[1,128]{1,0:T(1,128)S(1)}, u32[]{:S(2)}, u32[]{:S(2)}) collective-permute-start(f32[1,128]{1,0:T(1,128)S(1)} %get-tuple-element.246), channel_id=1, source_target_pairs={{0,16},{16,0},{1,17},{17,1},{2,18},{18,2},{3,19},{19,3},{4,20},{20... | collective-permute-start | bytes 1544 | tf_op jit(solution)/shard_map/ppermute | solution.py:255
  17.4 41.1 %collective-permute-start.7 = (bf16[18,768]{1,0:T(8,128)(2,1)}, bf16[18,768]{1,0:T(8,128)(2,1)}, u32[]{:S(2)}, u32[]{:S(2)}) collective-permute-start(bf16[18,768]{1,0:T(8,128)(2,1)} %pad_maximum_fusion.19), channel_id=1, source_target_pairs={{0,16},{16,0},{1,17},{17,1},{2,18},{18,2},{3,19},{19,3},{4,20},{20... | collective-permute-start | bytes 82952 | tf_op jit(solution)/shard_map/ppermute | solution.py:255
  18.1 29.9 %collective-permute-start = (bf16[128,768]{1,0:T(8,128)(2,1)}, bf16[128,768]{1,0:T(8,128)(2,1)}, u32[]{:S(2)}, u32[]{:S(2)}) collective-permute-start(bf16[128,768]{1,0:T(8,128)(2,1)} %get-tuple-element.237), channel_id=1, source_target_pairs={{0,16},{16,0},{1,17},{17,1},{2,18},{18,2},{3,19},{19,3},{4,20},{20... | collective-permute-start | bytes 589832 | tf_op jit(solution)/shard_map/ppermute | solution.py:255
  26.9 33.8 %collective-permute-start.3 = (bf16[192,1536]{1,0:T(8,128)(2,1)}, bf16[192,1536]{1,0:T(8,128)(2,1)}, u32[]{:S(2)}, u32[]{:S(2)}) collective-permute-start(bf16[192,1536]{1,0:T(8,128)(2,1)} %constant_dynamic-slice_fusion.2), channel_id=1, source_target_pairs={{0,16},{16,0},{1,17},{17,1},{2,18},{18,2},{3,19},{19,3},{4,20},{20... | collective-permute-start | bytes 1769480 | tf_op jit(solution)/shard_map/ppermute | solution.py:255
  60.7 21.3 %collective-permute-start.5 = (bf16[192,1536]{1,0:T(8,128)(2,1)}, bf16[192,1536]{1,0:T(8,128)(2,1)}, u32[]{:S(2)}, u32[]{:S(2)}) collective-permute-start(bf16[192,1536]{1,0:T(8,128)(2,1)} %collective-permute-done.3), channel_id=1, source_target_pairs={{0,1},{1,0},{2,3},{3,2},{4,5},{5,4},{6,7},{7,6},{8,9},{9,8},{10,11... | collective-permute-start | bytes 1769480 | tf_op jit(solution)/shard_map/ppermute | solution.py:224
  60.7 18.6 %collective-permute-start.4 = (bf16[192,1536]{1,0:T(8,128)(2,1)}, bf16[192,1536]{1,0:T(8,128)(2,1)}, u32[]{:S(2)}, u32[]{:S(2)}) collective-permute-start(bf16[192,1536]{1,0:T(8,128)(2,1)} %collective-permute-done.3), channel_id=1, source_target_pairs={{0,2},{1,3},{2,0},{3,1},{4,6},{5,7},{6,4},{7,5},{8,10},{9,11},{10,... | collective-permute-start | bytes 1769480 | tf_op jit(solution)/shard_map/ppermute | solution.py:224
  69.8 20.6 %collective-permute-start.9 = (bf16[768,512]{1,0:T(8,128)(2,1)S(1)}, bf16[768,512]{1,0:T(8,128)(2,1)}, u32[]{:S(2)}, u32[]{:S(2)}) collective-permute-start(bf16[768,512]{1,0:T(8,128)(2,1)S(1)} %get-tuple-element.66), channel_id=1, source_target_pairs={{0,16},{16,0},{1,17},{17,1},{2,18},{18,2},{3,19},{19,3},{4,20},{20... | collective-permute-start | bytes 2359304 | tf_op jit(solution)/shard_map/ppermute | solution.py:255
  71.6 35.7 %collective-permute-start.10 = (bf16[768,512]{1,0:T(8,128)(2,1)S(1)}, bf16[768,512]{1,0:T(8,128)(2,1)}, u32[]{:S(2)}, u32[]{:S(2)}) collective-permute-start(bf16[768,512]{1,0:T(8,128)(2,1)S(1)} %get-tuple-element.67), channel_id=1, source_target_pairs={{0,16},{16,0},{1,17},{17,1},{2,18},{18,2},{3,19},{19,3},{4,20},{20... | collective-permute-start | bytes 2359304 | tf_op jit(solution)/shard_map/ppermute | solution.py:255
  71.9 52.3 %collective-permute-start.11 = (bf16[256,1536]{1,0:T(8,128)(2,1)}, bf16[256,1536]{1,0:T(8,128)(2,1)}, u32[]{:S(2)}, u32[]{:S(2)}) collective-permute-start(bf16[256,1536]{1,0:T(8,128)(2,1)} %convert_bitcast_fusion), channel_id=1, source_target_pairs={{0,16},{16,0},{1,17},{17,1},{2,18},{18,2},{3,19},{19,3},{4,20},{20... | collective-permute-start | bytes 2359304 | tf_op jit(solution)/shard_map/ppermute | solution.py:255
  79.3 260.0 %collective-permute-start.71 = (bf16[128,768]{1,0:T(8,128)(2,1)}, bf16[128,768]{1,0:T(8,128)(2,1)}, u32[]{:S(2)}, u32[]{:S(2)}) collective-permute-start(bf16[128,768]{1,0:T(8,128)(2,1)} %get-tuple-element.233), channel_id=1, source_target_pairs={{0,16},{16,0},{1,17},{17,1},{2,18},{18,2},{3,19},{19,3},{4,20},{20... | collective-permute-start | bytes 589832 | tf_op jit(solution)/shard_map/ppermute | solution.py:255
  82.0 27.3 %collective-permute-start.6 = (bf16[192,1536]{1,0:T(8,128)(2,1)}, bf16[192,1536]{1,0:T(8,128)(2,1)S(1)}, u32[]{:S(2)}, u32[]{:S(2)}) collective-permute-start(bf16[192,1536]{1,0:T(8,128)(2,1)} %collective-permute-done.4), channel_id=1, source_target_pairs={{0,1},{1,0},{2,3},{3,2},{4,5},{5,4},{6,7},{7,6},{8,9},{9,8},{10,11... | collective-permute-start | bytes 1769480 | tf_op jit(solution)/shard_map/ppermute | solution.py:224
  127.1 38.6 %collective-permute-start.8 = (bf16[128,1536]{1,0:T(8,128)(2,1)S(1)}, bf16[128,1536]{1,0:T(8,128)(2,1)S(1)}, u32[]{:S(2)}, u32[]{:S(2)}) collective-permute-start(bf16[128,1536]{1,0:T(8,128)(2,1)S(1)} %multiply_convert_fusion.xa), channel_id=1, source_target_pairs={{0,1},{1,0},{2,3},{3,2},{4,5},{5,4},{6,7},{7,6},{8,9},{9,8},{10,11... | collective-permute-start | bytes 1179656 | tf_op jit(solution)/shard_map/ppermute | solution.py:221
  131.8 46.5 %collective-permute-start.24 = (bf16[256,1536]{1,0:T(8,128)(2,1)}, bf16[256,1536]{1,0:T(8,128)(2,1)}, u32[]{:S(2)}, u32[]{:S(2)}) collective-permute-start(bf16[256,1536]{1,0:T(8,128)(2,1)} %constant_dynamic-update-slice_fusion.6.xa), channel_id=1, source_target_pairs={{0,1},{1,0},{2,3},{3,2},{4,5},{5,4},{6,7},{7,6},{8,9},{9,8},{10,11... | collective-permute-start | bytes 2359304 | tf_op jit(solution)/shard_map/ppermute | solution.py:221
  150.8 39.9 %collective-permute-start.23 = (bf16[256,1536]{1,0:T(8,128)(2,1)}, bf16[256,1536]{1,0:T(8,128)(2,1)}, u32[]{:S(2)}, u32[]{:S(2)}) collective-permute-start(bf16[256,1536]{1,0:T(8,128)(2,1)} %constant_dynamic-update-slice_fusion.4.xa), channel_id=1, source_target_pairs={{0,1},{1,0},{2,3},{3,2},{4,5},{5,4},{6,7},{7,6},{8,9},{9,8},{10,11... | collective-permute-start | bytes 2359304 | tf_op jit(solution)/shard_map/ppermute | solution.py:221
  165.0 37.8 %collective-permute-start.22 = (bf16[256,1536]{1,0:T(8,128)(2,1)}, bf16[256,1536]{1,0:T(8,128)(2,1)}, u32[]{:S(2)}, u32[]{:S(2)}) collective-permute-start(bf16[256,1536]{1,0:T(8,128)(2,1)} %constant_dynamic-update-slice_fusion.2.xa), channel_id=1, source_target_pairs={{0,1},{1,0},{2,3},{3,2},{4,5},{5,4},{6,7},{7,6},{8,9},{9,8},{10,11... | collective-permute-start | bytes 2359304 | tf_op jit(solution)/shard_map/ppermute | solution.py:221
  166.5 48.0 %collective-permute-start.21 = (bf16[128,1536]{1,0:T(8,128)(2,1)}, bf16[128,1536]{1,0:T(8,128)(2,1)}, u32[]{:S(2)}, u32[]{:S(2)}) collective-permute-start(bf16[128,1536]{1,0:T(8,128)(2,1)} %constant_dynamic-update-slice_fusion.xa), channel_id=1, source_target_pairs={{0,1},{1,0},{2,3},{3,2},{4,5},{5,4},{6,7},{7,6},{8,9},{9,8},{10,11... | collective-permute-start | bytes 1179656 | tf_op jit(solution)/shard_map/ppermute | solution.py:221
  190.6 48.0 %collective-permute-start.31 = (bf16[256,1536]{1,0:T(8,128)(2,1)}, bf16[256,1536]{1,0:T(8,128)(2,1)S(1)}, u32[]{:S(2)}, u32[]{:S(2)}) collective-permute-start(bf16[256,1536]{1,0:T(8,128)(2,1)} %get-tuple-element.98), channel_id=1, source_target_pairs={{0,1},{1,0},{2,3},{3,2},{4,5},{5,4},{6,7},{7,6},{8,9},{9,8},{10,11... | collective-permute-start | bytes 2359304 | tf_op jit(solution)/shard_map/ppermute | solution.py:221
  202.3 37.2 %collective-permute-start.29 = (bf16[256,1536]{1,0:T(8,128)(2,1)}, bf16[256,1536]{1,0:T(8,128)(2,1)S(1)}, u32[]{:S(2)}, u32[]{:S(2)}) collective-permute-start(bf16[256,1536]{1,0:T(8,128)(2,1)} %get-tuple-element.96), channel_id=1, source_target_pairs={{0,1},{1,0},{2,3},{3,2},{4,5},{5,4},{6,7},{7,6},{8,9},{9,8},{10,11... | collective-permute-start | bytes 2359304 | tf_op jit(solution)/shard_map/ppermute | solution.py:221
  237.0 20.4 %collective-permute-start.91 = (bf16[768,512]{1,0:T(8,128)(2,1)S(1)}, bf16[768,512]{1,0:T(8,128)(2,1)S(1)}, u32[]{:S(2)}, u32[]{:S(2)}) collective-permute-start(bf16[768,512]{1,0:T(8,128)(2,1)S(1)} %dynamic-slice_convert_fusion.2), channel_id=1, source_target_pairs={{0,16},{16,0},{1,17},{17,1},{2,18},{18,2},{3,19},{19,3},{4,20},{20... | collective-permute-start | bytes 2359304 | tf_op jit(solution)/shard_map/ppermute | solution.py:255
  238.6 35.2 %collective-permute-start.93 = (bf16[256,1536]{1,0:T(8,128)(2,1)S(1)}, bf16[256,1536]{1,0:T(8,128)(2,1)S(1)}, u32[]{:S(2)}, u32[]{:S(2)}) collective-permute-start(bf16[256,1536]{1,0:T(8,128)(2,1)S(1)} %dynamic-slice_convert_fusion), channel_id=1, source_target_pairs={{0,16},{16,0},{1,17},{17,1},{2,18},{18,2},{3,19},{19,3},{4,20},{20... | collective-permute-start | bytes 2359304 | tf_op jit(solution)/shard_map/ppermute | solution.py:255
  246.3 242.6 %collective-permute-start.12 = (bf16[128,1536]{1,0:T(8,128)(2,1)S(1)}, bf16[128,1536]{1,0:T(8,128)(2,1)}, u32[]{:S(2)}, u32[]{:S(2)}) collective-permute-start(bf16[128,1536]{1,0:T(8,128)(2,1)S(1)} %copy-done.17), channel_id=1, source_target_pairs={{0,1},{1,0},{2,3},{3,2},{4,5},{5,4},{6,7},{7,6},{8,9},{9,8},{10,11... | collective-permute-start | bytes 1179656 | tf_op jit(solution)/shard_map/ppermute | solution.py:221
  248.6 28.1 %collective-permute-start.40 = (bf16[256,1664]{1,0:T(8,128)(2,1)S(1)}, bf16[256,1664]{1,0:T(8,128)(2,1)S(1)}, u32[]{:S(2)}, u32[]{:S(2)}) collective-permute-start(bf16[256,1664]{1,0:T(8,128)(2,1)S(1)} %get-tuple-element.104), channel_id=1, source_target_pairs={{0,1},{1,0},{2,3},{3,2},{4,5},{5,4},{6,7},{7,6},{8,9},{9,8},{10,11... | collective-permute-start | bytes 2555912 | tf_op jit(solution)/shard_map/ppermute | solution.py:221
  257.4 39.2 %collective-permute-start.44 = (bf16[256,1664]{1,0:T(8,128)(2,1)S(1)}, bf16[256,1664]{1,0:T(8,128)(2,1)S(1)}, u32[]{:S(2)}, u32[]{:S(2)}) collective-permute-start(bf16[256,1664]{1,0:T(8,128)(2,1)S(1)} %get-tuple-element.108), channel_id=1, source_target_pairs={{0,1},{1,0},{2,3},{3,2},{4,5},{5,4},{6,7},{7,6},{8,9},{9,8},{10,11... | collective-permute-start | bytes 2555912 | tf_op jit(solution)/shard_map/ppermute | solution.py:221
  338.0 34.4 %collective-permute-start.92 = (bf16[768,512]{1,0:T(8,128)(2,1)}, bf16[768,512]{1,0:T(8,128)(2,1)}, u32[]{:S(2)}, u32[]{:S(2)}) collective-permute-start(bf16[768,512]{1,0:T(8,128)(2,1)} %dynamic-slice_convert_fusion.1), channel_id=1, source_target_pairs={{0,16},{16,0},{1,17},{17,1},{2,18},{18,2},{3,19},{19,3},{4,20},{20... | collective-permute-start | bytes 2359304 | tf_op jit(solution)/shard_map/ppermute | solution.py:255
  339.4 79.3 %collective-permute-start.34 = (bf16[128,1536]{1,0:T(8,128)(2,1)}, bf16[128,1536]{1,0:T(8,128)(2,1)}, u32[]{:S(2)}, u32[]{:S(2)}) collective-permute-start(bf16[128,1536]{1,0:T(8,128)(2,1)} %pad_maximum_fusion.10), channel_id=1, source_target_pairs={{0,2},{1,3},{4,0},{5,1},{8,4},{9,5},{12,8},{13,9},{14,12},{15,13},... | collective-permute-start | bytes 1179656 | tf_op jit(solution)/shard_map/ppermute | solution.py:229
  346.6 21.3 %collective-permute-start.73 = (bf16[384,1536]{1,0:T(8,128)(2,1)}, bf16[384,1536]{1,0:T(8,128)(2,1)}, u32[]{:S(2)}, u32[]{:S(2)}) collective-permute-start(bf16[384,1536]{1,0:T(8,128)(2,1)} %slice.397), channel_id=1, source_target_pairs={{0,1},{1,0},{2,3},{3,2},{4,5},{5,4},{6,7},{7,6},{8,9},{9,8},{10,11... | collective-permute-start | bytes 3538952 | tf_op jit(solution)/shard_map/ppermute | solution.py:221
  382.1 37.3 %collective-permute-start.28 = (bf16[128,1536]{1,0:T(8,128)(2,1)S(1)}, bf16[128,1536]{1,0:T(8,128)(2,1)S(1)}, u32[]{:S(2)}, u32[]{:S(2)}) collective-permute-start(bf16[128,1536]{1,0:T(8,128)(2,1)S(1)} %pad_maximum_fusion.9), channel_id=1, source_target_pairs={{0,4},{1,5},{4,8},{5,9},{8,12},{9,13},{12,14},{13,15},{14,10},{15,... | collective-permute-start | bytes 1179656 | tf_op jit(solution)/shard_map/ppermute | solution.py:229
  437.8 47.8 %collective-permute-start.30 = (bf16[128,1536]{1,0:T(8,128)(2,1)S(1)}, bf16[128,1536]{1,0:T(8,128)(2,1)S(1)}, u32[]{:S(2)}, u32[]{:S(2)}) collective-permute-start(bf16[128,1536]{1,0:T(8,128)(2,1)S(1)} %get-tuple-element.224), channel_id=1, source_target_pairs={{0,4},{1,5},{4,8},{5,9},{8,12},{9,13},{12,14},{13,15},{14,10},{15,... | collective-permute-start | bytes 1179656 | tf_op jit(solution)/shard_map/ppermute | solution.py:229
  450.3 35.8 %collective-permute-start.35 = (bf16[128,1536]{1,0:T(8,128)(2,1)S(1)}, bf16[128,1536]{1,0:T(8,128)(2,1)S(1)}, u32[]{:S(2)}, u32[]{:S(2)}) collective-permute-start(bf16[128,1536]{1,0:T(8,128)(2,1)S(1)} %get-tuple-element.225), channel_id=1, source_target_pairs={{0,2},{1,3},{4,0},{5,1},{8,4},{9,5},{12,8},{13,9},{14,12},{15,13},... | collective-permute-start | bytes 1179656 | tf_op jit(solution)/shard_map/ppermute | solution.py:229
  467.1 20.0 %collective-permute-start.51 = (bf16[128,768]{1,0:T(8,128)(2,1)S(1)}, bf16[128,768]{1,0:T(8,128)(2,1)S(1)}, u32[]{:S(2)}, u32[]{:S(2)}) collective-permute-start(bf16[128,768]{1,0:T(8,128)(2,1)S(1)} %slice.485), channel_id=1, source_target_pairs={{0,16},{16,0},{1,17},{17,1},{2,18},{18,2},{3,19},{19,3},{4,20},{20... | collective-permute-start | bytes 589832 | tf_op jit(solution)/shard_map/ppermute | solution.py:255
  485.4 25.9 %collective-permute-start.70 = (bf16[384,2688]{1,0:T(8,128)(2,1)}, bf16[384,2688]{1,0:T(8,128)(2,1)}, u32[]{:S(2)}, u32[]{:S(2)}) collective-permute-start(bf16[384,2688]{1,0:T(8,128)(2,1)} %constant_dynamic-update-slice_fusion.8.own), channel_id=1, source_target_pairs={{0,1},{1,0},{2,3},{3,2},{4,5},{5,4},{6,7},{7,6},{8,9},{9,8},{10,11... | collective-permute-start | bytes 6193160 | tf_op jit(solution)/shard_map/ppermute | solution.py:221
  (166 other events, 1440.7 us)
Sparse Core Ops, SparseCore 0:
  14.7 66.5 all-gather.1

commit v2 on v1

v2 whole, which is shorter than its diff:
```python
import jax
import jax.numpy as jnp
import numpy as np
from jax import lax
from jax.experimental import pallas as pl
from jax.experimental.pallas import tpu as pltpu
from jax.sharding import PartitionSpec as P

HEAD = 64
norm_eps = 1e-06
score_scale = 0.015625
rope_base = 10000.0
mask_fill = -1e30
BF = jnp.bfloat16
F32 = jnp.float32


def narrow(v):
    return v.astype(BF)


def wide(v):
    return v.astype(F32)


def mm(a, b):
    return jnp.dot(a, b, preferred_element_type=F32)


def mm_tn(a, b):
    return lax.dot_general(a, b, (((0,), (0,)), ((), ())), preferred_element_type=F32)


def mm_nt(a, b):
    return lax.dot_general(a, b, (((1,), (1,)), ((), ())), preferred_element_type=F32)


def add_low(a, b):
    return narrow(wide(a) + wide(b))


def layout(lengths, length):
    pieces = lengths.shape[0]
    order = jnp.arange(pieces, dtype=jnp.int32)
    ends = jnp.sum(jnp.where(order[None, :] <= order[:, None], lengths[None, :], 0), 1)
    starts = ends - lengths
    at = jnp.arange(length, dtype=jnp.int32)
    segment = jnp.sum((at[:, None] >= ends[None, :]).astype(jnp.int32), 1)
    owned = segment[:, None] == order[None, :]
    places = at - jnp.sum(jnp.where(owned, starts[None, :], 0), 1)
    live = segment < pieces - 1
    allowed = (
        (segment[:, None] == segment[None, :])
        & (at[None, :] <= at[:, None])
        & (live[None, :] | (at[:, None] == at[None, :]))
    )
    return places, live, allowed


def tie(v, *after):
    return lax.optimization_barrier((v, *after))[0]


ANY = pl.BlockSpec(memory_space=pl.ANY)
BIG = pltpu.CompilerParams(vmem_limit_bytes=56 << 20)


def cost(flops, moved, hard=0):
    return pl.CostEstimate(flops=int(flops), bytes_accessed=int(moved), transcendentals=int(hard))


def like(*shape, dtype=BF):
    return jax.ShapeDtypeStruct(shape, dtype)


def load_parts(parts, spots, whole, sems):
    return [
        pltpu.make_async_copy(
            ref, whole.at[pl.ds(pl.multiple_of(spots[i], 16), ref.shape[0])], sems.at[i]
        )
        for i, ref in enumerate(parts)
    ]


def turn(v, cosine, sine):
    lane = lax.broadcasted_iota(jnp.int32, v.shape, 1) % HEAD
    other = jnp.where(lane < HEAD // 2, pltpu.roll(v, 96, 1), pltpu.roll(v, 32, 1))
    return v * cosine + other * sine


def twice(v, odd):
    low = lax.broadcasted_iota(jnp.int32, v.shape, 1) < HEAD
    return jnp.where(low != odd, v, pltpu.roll(v, HEAD, 1))


def softmax_rows(q3, keys, allowed3):
    s = jnp.where(allowed3, mm_nt(q3, keys) * score_scale, mask_fill)
    e = jnp.exp(s - jnp.max(s, -1, keepdims=True))
    return e / jnp.sum(e, -1, keepdims=True)


def project_columns(cols, inverses, gain, weights):
    length, dh = cols[0].shape
    widths = [w.shape[1] for w in weights]
    tile = 256
    counts = [w // tile for w in widths]
    first = [sum(counts[:i]) for i in range(len(counts))]
    total = sum(widths)

    def body(ca, cb, ia, ib, g, wq, wk, wv, own, other, normed, low):
        i = pl.program_id(0)

        @pl.when(i == 0)
        def _():
            gain_row = wide(narrow(g[...]))
            normed[:length] = narrow(wide(ca[...]) * ia[...] * gain_row)
            normed[length:] = narrow(wide(cb[...]) * ib[...] * gain_row)

        def go(w):
            low[...] = narrow(w[...])
            out = mm(normed[...], low[...])
            own[...], other[...] = out[:length], narrow(out[length:])

        for ref, a, n in zip((wq, wk, wv), first, counts):
            pl.when((i >= a) & (i < a + n))(lambda ref=ref: go(ref))

    whole = lambda a: pl.BlockSpec(a.shape, lambda i: (0, 0))
    column = lambda a, n: pl.BlockSpec((dh, tile), lambda i: (0, jnp.clip(i - a, 0, n - 1)))
    return pl.pallas_call(
        body,
        grid=(sum(counts),),
        in_specs=[whole(v) for v in (*cols, *inverses, gain)]
        + [column(a, n) for a, n in zip(first, counts)],
        out_specs=[
            pl.BlockSpec((length, tile), lambda i: (0, i)),
            pl.BlockSpec((length, tile), lambda i: (0, i)),
            pl.BlockSpec((2 * length, dh), lambda i: (0, 0)),
            pl.BlockSpec((dh, tile), lambda i: (0, i)),
        ],
        out_shape=[
            like(length, total, dtype=F32), like(length, total), like(2 * length, dh), like(dh, total),
        ],
        cost_estimate=cost(4 * length * dh * total, 6 * dh * total),
        name="project_columns",
    )(*cols, *inverses, gain, *weights)


def attend(sums, tables, tokens, gain_two, router, chosen, out_parts, out_spots, heads, kv_heads):
    length, width = tokens.shape
    group = heads // kv_heads
    fq, fk = heads * HEAD, kv_heads * HEAD
    total = fq + 2 * fk
    n_sum, n_out = len(sums), len(out_parts)

    def body(spots, *refs):
        parts, refs = refs[:n_sum], refs[n_sum:]
        cosine, sine, allowed, live, tok, gain, rt, pick = refs[:8]
        outs = refs[8 : 8 + n_out]
        qkv_o, att_o, mid_o, norm_o, gate_o, w_out, sems = refs[8 + n_out :]
        copies = load_parts(outs, spots, w_out, sems)
        for copy in copies:
            copy.start()
        cos, sin = cosine[...], sine[...]

        def block(j):
            at = slice(j * 128, j * 128 + 128)
            v = wide(parts[0][:, at])
            for p in parts[1:]:
                v = v + wide(p[:, at])
            return at, v

        keys, values, q = [], [], []
        for j in range(fq // 128):
            at, v = block(j)
            v = narrow(turn(v, cos, sin))
            qkv_o[:, at] = v
            q.append(v)
        for j in range(fk // 128):
            at, v = block(fq // 128 + j)
            v = turn(v, cos, sin)
            qkv_o[:, at] = narrow(v)
            keys += [narrow(twice(v, False)), narrow(twice(v, True))]
        for j in range(fk // 128):
            at, v = block((fq + fk) // 128 + j)
            qkv_o[:, at] = narrow(v)
            values += [narrow(twice(v, False)), narrow(twice(v, True))]
        low = lax.broadcasted_iota(jnp.int32, (length, 128), 1) < HEAD
        ok = jnp.concatenate([allowed[...] > 0] * group)
        alive = live[...] > 0
        done = {}
        zero = jnp.zeros((length, 128), BF)
        for g in range(kv_heads):
            hs = range(g * group, (g + 1) * group)
            q3 = jnp.concatenate([jnp.where(low != bool(h % 2), q[h // 2], zero) for h in hs])
            a = narrow(softmax_rows(q3, keys[g], ok))
            ctx = mm(a, values[g])
            for n, h in enumerate(hs):
                done[h] = ctx[n * length : (n + 1) * length]
                if h % 2:
                    both = jnp.where(low, done.pop(h - 1), done.pop(h))
                    att_o[:, h // 2 * 128 : h // 2 * 128 + 128] = narrow(
                        jnp.where(alive, both, 0.0)
                    )
        for copy in copies:
            copy.wait()
        mid = wide(tok[...]) + mm(att_o[...], w_out[...])
        mid_o[...] = mid
        inverse = lax.rsqrt(jnp.mean(mid * mid, -1, keepdims=True) + norm_eps)
        normed = narrow(mid * inverse * gain[...])
        norm_o[...] = normed
        yes = pick[...] > 0
        logits = jnp.where(yes, mm_nt(normed, rt[...]), mask_fill)
        up = jnp.where(yes, jnp.exp(logits - jnp.max(logits, -1, keepdims=True)), 0.0)
        gate_o[...] = up / jnp.sum(up, -1, keepdims=True)

    given = (*sums, *tables, tokens, gain_two, router, chosen)
    whole = [pl.BlockSpec(memory_space=pltpu.VMEM)] * len(given)
    return pl.pallas_call(
        body,
        in_specs=[pl.BlockSpec(memory_space=pltpu.SMEM)] + whole + [ANY] * n_out,
        out_shape=[
            like(length, total),
            like(length, fq),
            like(length, width, dtype=F32),
            like(length, width),
            like(length, router.shape[0], dtype=F32),
        ],
        scratch_shapes=[
            pltpu.VMEM((fq, width), BF),
            pltpu.SemaphoreType.DMA((n_out,)),
        ],
        compiler_params=BIG,
        cost_estimate=cost(
            2 * length * fq * width + 4 * heads * length * length * 128,
            2 * fq * width + 12 * length * total,
            heads * length * length,
        ),
        name="attend",
    )(out_spots, *given, *out_parts)


def second_norm_back(sums, gates, router, mid, gain_two, cotangent, normed, experts):
    length, width = mid.shape
    tail = router.shape[0]

    def body(a, b, c, gate_r, rt, mid_r, gain, cot, norm, mid_o, branch_o, small_o):
        ends = wide(a[:, width:]) + wide(b[:, width:]) + wide(c[:, width:])
        grad = ends + pltpu.roll(ends, tail // 2, 1)
        gate = gate_r[...]
        chosen = gate * (grad - jnp.sum(gate * grad, -1, keepdims=True))
        logit = narrow(chosen)
        n2g = wide(a[:, :width]) + wide(b[:, :width]) + wide(c[:, :width]) + mm(logit, rt[...])
        m = mid_r[...]
        inverse = lax.rsqrt(jnp.mean(m * m, -1, keepdims=True) + norm_eps)
        scaled = m * inverse
        du = n2g * gain[...]
        out = wide(cot[...]) + inverse * (
            du - scaled * jnp.mean(du * scaled, -1, keepdims=True)
        )
        mid_o[...] = out
        branch_o[...] = narrow(out)
        small_o[:experts] = narrow(mm_tn(logit, norm[...])[:experts])
        gain_row = jnp.sum(n2g * scaled, 0, keepdims=True)
        small_o[experts:] = narrow(jnp.broadcast_to(gain_row, (16, width)))

    return pl.pallas_call(
        body,
        out_shape=[like(length, width, dtype=F32), like(length, width), like(experts + 16, width)],
        compiler_params=BIG,
        cost_estimate=cost(6 * length * width * tail, 20 * length * width),
        name="second_norm_back",
    )(*sums, gates, router, mid, gain_two, cotangent, normed)


def attend_back(qkv, tables, branch, out_parts, out_spots, heads, kv_heads):
    length, width = branch.shape
    group = heads // kv_heads
    fq, fk = heads * HEAD, kv_heads * HEAD
    total = fq + 2 * fk
    n_out = len(out_parts)

    def body(spots, qkv_r, cosine, sine, allowed, live, br, *refs):
        outs = refs[:n_out]
        grads, w_out, sems = refs[n_out:]
        copies = load_parts(outs, spots, w_out, sems)
        for copy in copies:
            copy.start()
        cos, sin = cosine[...], -sine[...]
        low = lax.broadcasted_iota(jnp.int32, (length, 128), 1) < HEAD
        ok = jnp.concatenate([allowed[...] > 0] * group)
        zero = jnp.zeros((length, 128), BF)
        q = [qkv_r[:, j * 128 : j * 128 + 128] for j in range(fq // 128)]
        keys, values = [], []
        for store, base in ((keys, fq), (values, fq + fk)):
            for j in range(fk // 128):
                v = wide(qkv_r[:, base + j * 128 : base + j * 128 + 128])
                store += [narrow(twice(v, False)), narrow(twice(v, True))]
        for copy in copies:
            copy.wait()
        cg = narrow(jnp.where(live[...] > 0, mm_nt(br[...], w_out[...]), 0.0))
        done, fold = {}, {}

        def put(at, v, rotate):
            v = turn(v, cos, sin) if rotate else v
            grads[:, at * 128 : at * 128 + 128] = narrow(v)

        for g in range(kv_heads):
            hs = range(g * group, (g + 1) * group)
            pick = lambda src: jnp.concatenate(
                [jnp.where(low != bool(h % 2), src(h // 2), zero) for h in hs]
            )
            q3 = pick(lambda j: q[j])
            c3 = pick(lambda j: cg[:, j * 128 : j * 128 + 128])
            a = softmax_rows(q3, keys[g], ok)
            ag = mm_nt(c3, values[g])
            sg = narrow(a * (ag - jnp.sum(a * ag, -1, keepdims=True)))
            vg = mm_tn(narrow(a), c3)
            kg = score_scale * mm_tn(sg, q3)
            qg = score_scale * mm(sg, keys[g])
            fold[g] = (kg + pltpu.roll(kg, HEAD, 1), vg + pltpu.roll(vg, HEAD, 1))
            for n, h in enumerate(hs):
                done[h] = qg[n * length : (n + 1) * length]
                if h % 2:
                    put(h // 2, jnp.where(low, done.pop(h - 1), done.pop(h)), True)
            if g % 2:
                (ka, va), (kb, vb) = fold.pop(g - 1), fold.pop(g)
                put(fq // 128 + g // 2, jnp.where(low, ka, kb), True)
                put((fq + fk) // 128 + g // 2, jnp.where(low, va, vb), False)

    vm = pl.BlockSpec(memory_space=pltpu.VMEM)
    return pl.pallas_call(
        body,
        in_specs=[pl.BlockSpec(memory_space=pltpu.SMEM)] + [vm] * 6 + [ANY] * n_out,
        out_shape=like(length, total),
        scratch_shapes=[pltpu.VMEM((fq, width), BF), pltpu.SemaphoreType.DMA((n_out,))],
        compiler_params=BIG,
        cost_estimate=cost(
            2 * length * fq * width + 12 * heads * length * length * 128,
            2 * fq * width + 8 * length * total,
            heads * length * length,
        ),
        name="attend_back",
    )(out_spots, qkv, *tables, branch, *out_parts)


def ring_rows(wanted, at, value, scratch, own, sib, columns):
    per = value.shape[0] // wanted
    scratch[...] = value
    for i in range(wanted):
        block = narrow(scratch[pl.ds(pl.multiple_of(at[i] * per, 8), per)])
        out, j = (own, i) if i < wanted // 2 else (sib, i - wanted // 2)
        out[j * per : (j + 1) * per, columns] = block


def out_gradient(attended, branches, seats):
    dh, width = attended[0].shape[1], branches[0].shape[1]
    tile = 512

    def body(at, aa, ab, ba, bb, own, sib, scratch):
        a = jnp.concatenate([aa[...], ab[...]])
        b = jnp.concatenate([ba[...], bb[...]])
        for j in range(width // tile):
            cols = slice(j * tile, (j + 1) * tile)
            ring_rows(seats.shape[0], at, mm_tn(a, b[:, cols]), scratch, own, sib, cols)

    vm = pl.BlockSpec(memory_space=pltpu.VMEM)
    return pl.pallas_call(
        body,
        in_specs=[pl.BlockSpec(memory_space=pltpu.SMEM)] + [vm] * 4,
        out_shape=[like(dh // 2, width)] * 2,
        scratch_shapes=[pltpu.VMEM((dh, tile), F32)],
        compiler_params=BIG,
        cost_estimate=cost(4 * attended[0].shape[0] * dh * width, 2 * dh * width),
        name="out_gradient",
    )(seats, *attended, *branches)


def projection_gradient(grads, low, normed, cols, inverses, small, seats, experts):
    length, total = grads[0].shape
    dh = low.shape[0]
    tile = 256
    steps = total // tile

    def body(at, ga, gb, w, norm, ca, cb, ia, ib, sa, sb, own, sib, n1a, n1b, scratch, acc, last):
        i = pl.program_id(0)
        g = jnp.concatenate([ga[...], gb[...]])
        add = mm_nt(g, w[...])

        @pl.when(i == 0)
        def _():
            acc[...] = add

        @pl.when(i > 0)
        def _():
            acc[...] += add

        where = pl.ds(pl.multiple_of(i * tile, tile), tile)
        ring_rows(seats.shape[0], at, mm_tn(norm[...], g), scratch, own, sib, where)

        @pl.when(i == steps - 1)
        def _():
            n1 = acc[...]
            n1a[...], n1b[...] = n1[:length], narrow(n1[length:])
            gain = n1[:length] * (wide(ca[...]) * ia[...]) + n1[length:] * (
                wide(cb[...]) * ib[...]
            )
            last[...] = jnp.zeros_like(last)
            last[: experts + 16] = wide(sa[...]) + wide(sb[...])
            row = jnp.sum(gain, 0, keepdims=True)
            last[experts + 8 : experts + 16] = jnp.broadcast_to(row, (8, dh))
            ring_rows(
                seats.shape[0], at, last[...].T, scratch.at[:, :128], own, sib,
                slice(total, total + 128),
            )

    whole = lambda a: pl.BlockSpec(a.shape, lambda i, at: (0, 0))
    column = lambda a: pl.BlockSpec((a.shape[0], tile), lambda i, at: (0, i))
    shapes = [like(dh // 2, total + 128)] * 2 + [like(length, dh, dtype=F32), like(length, dh)]
    return pl.pallas_call(
        body,
        grid_spec=pltpu.PrefetchScalarGridSpec(
            num_scalar_prefetch=1,
            grid=(steps,),
            in_specs=[column(grads[0]), column(grads[1]), column(low)]
            + [whole(v) for v in (normed, *cols, *inverses, *small)],
            out_specs=[whole(s) for s in shapes],
            scratch_shapes=[
                pltpu.VMEM((dh, tile), F32),
                pltpu.VMEM((2 * length, dh), F32),
                pltpu.VMEM((128, dh), F32),
            ],
        ),
        out_shape=shapes,
        compiler_params=BIG,
        cost_estimate=cost(8 * length * dh * total, 4 * dh * total),
        name="projection_gradient",
    )(seats, *grads, low, normed, *cols, *inverses, *small)


def put_rows(pair, at, widths):
    rows, per = pair[0].shape[0] * 2, pair[0].shape[0] * 2 // at.shape[0]
    n = at.shape[0]
    c = n // 2
    total = sum(widths)
    cuts = [sum(widths[:i]) for i in range(len(widths) + 1)]
    if per % 16:
        out = jnp.zeros((rows, total), F32)
        for i in range(n):
            blk = wide(pair[i // c][i % c * per : (i % c + 1) * per])
            out = lax.dynamic_update_slice_in_dim(out, blk, at[i] * per, 0)
        return [out[:, a:b] for a, b in zip(cuts, cuts[1:])]
    k = len(widths)

    def body(at_ref, own, sib, *refs):
        outs, held, sems = refs[:k], refs[k : 2 * k], refs[2 * k]
        copies = []
        for i in range(n):
            src, j = (own, i) if i < c else (sib, i - c)
            row = pl.multiple_of(at_ref[i] * per, 8)
            for w in range(k):
                held[w][i * per : (i + 1) * per] = wide(
                    src[j * per : (j + 1) * per, cuts[w] : cuts[w + 1]]
                )
                copy = pltpu.make_async_copy(
                    held[w].at[pl.ds(i * per, per)], outs[w].at[pl.ds(row, per)], sems.at[i, w]
                )
                copy.start()
                copies.append(copy)
        for copy in copies:
            copy.wait()

    vm = pl.BlockSpec(memory_space=pltpu.VMEM)
    return pl.pallas_call(
        body,
        in_specs=[pl.BlockSpec(memory_space=pltpu.SMEM), vm, vm],
        out_specs=[ANY] * k,
        out_shape=[like(rows, w, dtype=F32) for w in widths],
        scratch_shapes=[pltpu.VMEM((rows, w), F32) for w in widths]
        + [pltpu.SemaphoreType.DMA((n, k))],
        compiler_params=BIG,
        cost_estimate=cost(rows * total, rows * total * 6),
        name="put_rows",
    )(at, *pair)


def expert_step(me, tiles, cots, cot_blocks, router, gate, up, down, spots, kept, start, total):
    width, ffe = cots.shape[1] - router.shape[0], gate[0].shape[1]
    tail = router.shape[0]
    count = len(tiles)
    two = sum(p.shape[0] for p in tiles[0])
    block = two // 2
    n = count * block
    pieces = [p for t in tiles for p in t]
    parts = [*gate, *up, *down]
    k, m = len(gate), len(pieces)

    def body(spot, rows_at, ca, cb, rt, *refs):
        xs, ws = refs[:m], refs[m : m + 3 * k]
        refs = refs[-15:]
        mix_a, mix_b, row_a, row_b, x_o, hid_o, gpg_o, upg_o, rg_o = refs[:9]
        held, gw, uw, dw, sems, wsems = refs[9:]
        i = pl.program_id(0)
        moves, at, j = [], 0, 0
        for t in tiles:
            group = []
            for p in t:
                dst = held.at[pl.ds(at, p.shape[0])]
                group.append(pltpu.make_async_copy(xs[j], dst, sems.at[j]))
                at, j = at + p.shape[0], j + 1
            moves.append(group)
        loads = []
        for z, whole in enumerate((gw, uw, dw)):
            loads.append(
                [
                    pltpu.make_async_copy(
                        ws[z * k + p],
                        whole.at[
                            pl.ds(pl.multiple_of(rows_at[z * k + p], 16), ws[z * k + p].shape[0])
                        ],
                        wsems.at[z * k + p],
                    )
                    for p in range(k)
                ]
            )

        @pl.when(i == 0)
        def _():
            for copy in [*moves[0], *loads[0], *loads[1], *loads[2]]:
                copy.start()
            for copy in [c for g in moves[1:] for c in g]:
                copy.start()

        for t in range(count):

            @pl.when(i == t)
            def _():
                for copy in moves[t]:
                    copy.wait()

        @pl.when(i == 0)
        def _():
            for copy in [*loads[0], *loads[1], *loads[2]]:
                copy.wait()

        x = held[pl.ds(pl.multiple_of(i * two, two), two)]
        cm = jnp.concatenate([ca[...], cb[...]])
        cot, chosen = wide(cm[:, :width]), cm[:, width:] > 0
        x_o[...] = x
        logits = jnp.where(chosen, mm_nt(x, rt[...]), mask_fill)
        top = jnp.max(logits, -1, keepdims=True)
        raised = jnp.where(chosen, jnp.exp(logits - top), 0.0)
        mine = lax.broadcasted_iota(jnp.int32, raised.shape, 1)
        weight = jnp.sum(jnp.where(mine == spot[0], raised, 0.0), -1, keepdims=True)
        weight = wide(narrow(weight / jnp.sum(raised, -1, keepdims=True)))
        gate_pre, up_pre = mm(x, gw[...]), mm(x, uw[...])
        sg = jax.nn.sigmoid(gate_pre)
        silu = gate_pre * sg
        hidden = narrow(silu * up_pre)
        hid_o[...] = hidden
        result_grad = narrow(weight * cot)
        rg_o[...] = result_grad
        result = wide(narrow(mm(hidden, dw[...])))
        mix = narrow(weight * result)
        mix_a[...], mix_b[...] = mix[:block], mix[block:]
        gate_grad = jnp.sum(result * cot, -1, keepdims=True)
        hidden_grad = mm_nt(result_grad, dw[...])
        gpg = narrow(hidden_grad * up_pre * sg * (1.0 + gate_pre * (1.0 - sg)))
        upg = narrow(hidden_grad * silu)
        gpg_o[...], upg_o[...] = gpg, upg
        row = narrow(mm_nt(gpg, gw[...]) + mm_nt(upg, uw[...]))
        row_a[:, :width], row_b[:, :width] = row[:block], row[block:]
        high = wide(narrow(gate_grad))
        ends = jnp.where(mine == spot[0], high, 0.0)
        ends = narrow(jnp.where(mine == spot[0] + tail // 2, gate_grad - high, ends))
        row_a[:, width:], row_b[:, width:] = ends[:block], ends[block:]

    step = lambda w: pl.BlockSpec((block, w), lambda i, s, r: (i, 0))
    keep = lambda w: pl.BlockSpec((two, w), lambda i, s, r: (start + i, 0))
    widths = [width, ffe, ffe, ffe, width]
    out_shape = [like(n, width), like(n, width), like(n, width + tail), like(n, width + tail)]
    out_shape += [like(total, w) for w in widths]
    given = list(kept or ())
    before = 5 + m + 3 * k
    return pl.pallas_call(
        body,
        grid_spec=pltpu.PrefetchScalarGridSpec(
            num_scalar_prefetch=2,
            grid=(count,),
            in_specs=[
                pl.BlockSpec((block, width + tail), lambda i, s, r: (s[1 + i], 0)),
                pl.BlockSpec((block, width + tail), lambda i, s, r: (s[1 + count + i], 0)),
                pl.BlockSpec(router.shape, lambda i, s, r: (0, 0)),
            ]
            + [ANY] * (m + 3 * k + len(given)),
            out_specs=[step(width), step(width), step(width + tail), step(width + tail)]
            + [keep(w) for w in widths],
            scratch_shapes=[
                pltpu.VMEM((count * two, width), BF),
                pltpu.VMEM((width, ffe), BF),
                pltpu.VMEM((width, ffe), BF),
                pltpu.VMEM((ffe, width), BF),
                pltpu.SemaphoreType.DMA((m,)),
                pltpu.SemaphoreType.DMA((3 * k,)),
            ],
        ),
        out_shape=out_shape,
        input_output_aliases={before + i: 4 + i for i in range(len(given))},
        compiler_params=BIG,
        cost_estimate=cost(
            24 * n * width * ffe, 6 * width * ffe + n * width * 28, 2 * n * ffe
        ),
        name="expert_step",
    )(jnp.stack([me, *cot_blocks]).astype(jnp.int32), spots, cots, cots, router, *pieces, *parts, *given)


class Links:
    def __init__(self):
        self.n = lax.axis_size("dp")
        self.e = lax.axis_size("expert")
        self.chips = self.e // 2
        order = list(range(self.chips))
        if self.n == 2 and self.chips == 8:
            order = [0, 2, 4, 6, 7, 5, 3, 1]
        self.order = order
        where = np.argsort(np.array(order)).astype(np.int32)
        self.x = lax.axis_index("dp")
        self.me = lax.axis_index("expert")
        self.core = self.me % 2
        chip = self.me // 2
        self.place = jnp.sum(
            jnp.where(jnp.arange(self.chips, dtype=jnp.int32) == chip, jnp.asarray(where), 0)
        )

    def at_place(self, r):
        return (self.place + r) % self.chips

    def at(self, r, lane):
        place = self.at_place(r)
        order = jnp.asarray(np.array(self.order, np.int32))
        chip = jnp.sum(jnp.where(jnp.arange(self.chips, dtype=jnp.int32) == place, order, 0))
        return chip * 2 + (self.core ^ lane)

    def sibling(self, v):
        return lax.ppermute(v, "expert", [(i, i ^ 1) for i in range(self.e)])

    def flip(self, v, bit):
        return lax.ppermute(v, "expert", [(i, i ^ bit) for i in range(self.e)])

    def ring(self, v, step):
        c, o = self.chips, self.order
        pairs = [(o[k] * 2 + l, o[(k + step) % c] * 2 + l) for k in range(c) for l in (0, 1)]
        return lax.ppermute(v, "expert", pairs)

    def gather(self, block):
        c = self.chips
        half = block.shape[0] // 2
        got = {0: block}
        up = down = block
        for s in range(1, c // 2):
            up, down = self.ring(up, 1), self.ring(down, -1)
            got[c - s], got[s] = up, down
        far = (self.ring(up[:half], 1), self.ring(down[half:], -1))
        return got, far

    def scatter(self, s, far):
        c = self.chips
        half = far[0].shape[0]
        first = up, down = self.ring(far[0], 1), self.ring(far[1], -1)
        r = c // 2 - 1
        up = jnp.concatenate([add_low(up, s[r][:half]), s[r][half:]])
        down = jnp.concatenate([s[c - r][:half], add_low(down, s[c - r][half:])])
        up, down = self.ring(up, 1), self.ring(down, -1)
        for r in range(c // 2 - 2, 0, -1):
            up, down = self.ring(add_low(up, s[r]), 1), self.ring(add_low(down, s[c - r]), -1)
        return (s[0], up, down), first

    def swap(self, v):
        return lax.ppermute(v, "dp", [(0, 1), (1, 0)])

    def pick(self, v, other, axis):
        size = v.shape[axis] // self.n
        at = (1 - self.x if other else self.x) * size
        return lax.dynamic_slice_in_dim(v, at, size, axis)

    def both(self, own, got, axis):
        return jnp.where(
            self.x == 0,
            jnp.concatenate([own, got], axis),
            jnp.concatenate([got, own], axis),
        )

    def columns(self, v):
        if self.n == 2:
            return jnp.concatenate([self.pick(v, False, 1), self.swap(self.pick(v, True, 1))])
        return lax.all_to_all(v, "dp", split_axis=1, concat_axis=0, tiled=True)

    def columns_back(self, v):
        if self.n == 2:
            t = v.shape[0] // 2
            return self.both(v[:t], wide(self.swap(narrow(v[t:]))), 1)
        return wide(lax.all_to_all(narrow(v), "dp", split_axis=0, concat_axis=1, tiled=True))

    def rows(self, v):
        if self.n == 2:
            return jnp.concatenate([v, self.swap(v)])
        return lax.all_gather(v, "dp", axis=0, tiled=True)

    def sum_back(self, v):
        if self.n == 2:
            t = v.shape[0] // 2
            return v[:t] + wide(self.swap(narrow(v[t:])))
        return wide(lax.psum_scatter(narrow(v), "dp", scatter_dimension=0, tiled=True))

    def whole(self, v, axis):
        if self.n == 2:
            return self.both(v, self.swap(v), axis)
        return lax.all_gather(v, "dp", axis=axis, tiled=True)

    def shard_sum(self, v, axis, after=None):
        if self.n == 2:
            got = self.swap(narrow(self.pick(v, True, axis)))
            return self.pick(v, False, axis) + wide(got if after is None else tie(got, after))
        return wide(lax.psum_scatter(narrow(v), "dp", scatter_dimension=axis, tiled=True))

    def parts(self, w):
        if self.n == 2:
            n = w.shape[0]
            return [w, self.swap(w)], [self.x * n, (1 - self.x) * n]
        return [lax.all_gather(w, "dp", axis=0, tiled=True)], [self.x * 0]

    def parts_by_four(self, w):
        if self.n != 2 or self.e % 4:
            return self.parts(w)
        n = w.shape[0]
        part = n // 4
        q = self.me % 4
        a = self.swap(lax.dynamic_slice_in_dim(w, q * part, part, 0))
        b = self.flip(a, 2)
        c, d = self.flip(a, 1), self.flip(b, 1)
        base = (1 - self.x) * n
        return [w, a, b, c, d], [self.x * n] + [base + (q ^ z) * part for z in (0, 2, 1, 3)]


def wide_sum(v):
    out = wide(v[0])
    for w in v[1:]:
        out = out + wide(w)
    return out


def shards(
    tokens, cotangent, lengths, routes, gain_attn, w_query, key_weight, value_weight,
    w_out, gain_moe, w_router, w_gate, w_up, w_down,
):
    net = Links()
    c, pair = net.chips, net.n == 2
    length, width = tokens.shape
    dh = gain_attn.shape[0]
    heads, kv_heads = w_query.shape[1] // HEAD, key_weight.shape[1] // HEAD
    fq, fk = w_query.shape[1], key_weight.shape[1]
    experts = w_router.shape[1]
    tail = 128
    far, half = c // 2, length // 2

    stream = wide(tokens)
    inv_one = lax.rsqrt(jnp.mean(stream * stream, -1, keepdims=True) + norm_eps)
    if pair:
        cols = (net.pick(tokens, False, 1), net.swap(net.pick(tokens, True, 1)))
        inverses = (inv_one, net.swap(inv_one.reshape(1, length)).reshape(length, 1))
        own, other, normed_cols, w_qkv = project_columns(
            cols, inverses, gain_attn[None], (w_query, key_weight, value_weight)
        )
        arrived = net.swap(other)
        sums = (own, arrived)
    else:
        scaled_cols = wide(net.columns(tokens)) * net.rows(inv_one.reshape(1, length)).reshape(-1, 1)
        normed_cols = narrow(scaled_cols * wide(narrow(gain_attn))[None, :])
        w_qkv = jnp.concatenate([narrow(w_query), narrow(key_weight), narrow(value_weight)], 1)
        arrived = net.sum_back(mm(normed_cols, w_qkv))
        sums = (arrived,)

    small = jnp.concatenate(
        [narrow(w_router).T, narrow(gain_attn)[None], narrow(gain_moe)[None]], 0
    )
    small = net.whole(small, 1)
    gain_one, gain_two = wide(small[experts])[None], wide(small[experts + 1])[None]
    router = jnp.pad(small[:experts], ((0, tail - experts), (0, 0)))
    out_parts, out_spots = net.parts_by_four(narrow(w_out))
    out_spots = jnp.stack(out_spots).astype(jnp.int32)
    hits = routes[:, :, None] == jnp.arange(tail, dtype=jnp.int32)[None, None, :]
    chosen = narrow(jnp.any(hits, 1))
    cot_all = lax.all_gather(
        jnp.concatenate([cotangent, chosen], 1), "expert", axis=0, tiled=True
    )
    gate_parts, gate_spots = net.parts(tie(narrow(w_gate[0]), arrived))
    up_parts, _ = net.parts(tie(narrow(w_up[0]), arrived))
    down_parts, down_spots = net.parts(tie(narrow(w_down[0]), arrived))
    expert_spots = jnp.stack(gate_spots * 2 + down_spots).astype(jnp.int32)

    places, live, allowed = layout(lengths[0], length)
    inner = jnp.arange(128, dtype=jnp.int32) % (HEAD // 2)
    angles = places.astype(F32)[:, None] * (rope_base ** (-inner.astype(F32) * 2.0 / HEAD))[None]
    sign = jnp.where(jnp.arange(128) % HEAD < HEAD // 2, -1.0, 1.0)[None]
    tables = (
        jnp.cos(angles), jnp.sin(angles) * sign, allowed.astype(F32), live.astype(F32)[:, None],
    )
    qkv, attended, mid, normed_two, gates = attend(
        sums, tables, tokens, gain_two, router, chosen, out_parts, out_spots, heads, kv_heads
    )

    got, ends = net.gather(normed_two)
    beside = {r: net.sibling(v) for r, v in got.items()}
    ends_beside = tuple(net.sibling(v) for v in ends)
    near = [0] + [r for s in range(1, far - 1) for r in (s, c - s)]
    kept, start, mixes, backs = None, 0, {}, {}
    for g in (near, [far, far - 1, c - far + 1]):
        tiles = [(*ends, *ends_beside) if r == far else (got[r], beside[r]) for r in g]
        blocks = [net.at(r, l) for l in (0, 1) for r in g]
        out = expert_step(
            net.me, tiles, cot_all, blocks, router, gate_parts, up_parts, down_parts,
            expert_spots, kept, start, net.e * length,
        )
        kept, start = out[4:], start + len(g)
        for store, a, b in ((mixes, out[0], out[1]), (backs, out[2], out[3])):
            s = add_low(a, net.sibling(b))
            for i, r in enumerate(g):
                store[r] = s[i * length : (i + 1) * length]
        if g == near:
            after_near = out[0]
    back, first = net.scatter(backs, (backs[far][:half], backs[far][half:]))
    mix_far = tie(mixes[far], back[1])
    mixed, _ = net.scatter(mixes, (mix_far[:half], mix_far[half:]))
    mixed = narrow(mid + wide_sum(mixed))

    rows_all, hid_all, gpg_all, upg_all, rg_all = kept
    hid_all, gpg_all, upg_all = (tie(v, first[0]) for v in (hid_all, gpg_all, upg_all))
    expert_grads = [mm_tn(hid_all, rg_all), mm_tn(rows_all, gpg_all), mm_tn(rows_all, upg_all)]

    mid_grad, branch, d_small = second_norm_back(
        back, gates, router, mid, gain_two, cotangent, normed_two, experts
    )

    seats = jnp.stack([net.at_place(r) * 2 + (net.core ^ l) for l in (0, 1) for r in range(c)])
    seats = seats.astype(jnp.int32)
    per = dh // net.e
    if not pair:
        slot = jnp.arange(dh, dtype=jnp.int32)
        source = jnp.sum(
            jnp.where(slot[:, None] // per == jnp.arange(net.e)[None, :], seats[None, :], 0), 1
        ) * per + slot % per
        perm = (slot[:, None] == source[None, :]).astype(BF)

    def all_sum(own, sib, widths):
        s = add_low(own, net.sibling(sib))
        s = {r: s[r * per : (r + 1) * per] for r in range(c)}
        cut = per // 2
        total, _ = net.scatter(s, (s[far][:cut], s[far][cut:]))
        got, ends = net.gather(narrow(wide_sum(total)))
        got[far] = jnp.concatenate(ends)
        own = jnp.concatenate([got[r] for r in range(c)])
        return put_rows((own, net.sibling(own)), seats, widths)

    if pair:
        part = tie(net.pick(attended, True, 1), after_near)
        pieces = out_gradient(
            (net.pick(attended, False, 1), net.swap(part)), (branch, net.swap(branch)), seats
        )
    else:
        d = narrow(mm_tn(narrow(mm(net.columns(attended), perm)), net.rows(branch)))
        pieces = d[: dh // 2], d[dh // 2 :]
    [d_out] = all_sum(*pieces, [width])

    grads = attend_back(qkv, tables, branch, out_parts, out_spots, heads, kv_heads)
    if pair:
        d_small = (net.pick(d_small, False, 1), net.swap(net.pick(d_small, True, 1)))
        own, sib, n1, n1_other = projection_gradient(
            (grads, net.swap(grads)), w_qkv, normed_cols, cols, inverses, d_small, seats, experts
        )
        n1g = net.both(n1, wide(net.swap(n1_other)), 1)
    else:
        grads_all = net.rows(grads)
        d_qkv = mm_tn(narrow(mm(normed_cols, perm)), grads_all)
        n1 = mm_nt(grads_all, w_qkv)
        n1g = net.columns_back(n1)
        d_small = net.shard_sum(wide(d_small), 1)
        d_gain = jnp.broadcast_to(jnp.sum(n1 * scaled_cols, 0)[None], (8, dh))
        d_small = jnp.concatenate([d_small[: experts + 8], d_gain], 0)
        d_small = jnp.pad(mm(narrow(d_small), perm).T, ((0, 0), (0, tail - experts - 16)))
        d = narrow(jnp.concatenate([d_qkv, d_small], 1))
        own, sib = d[: dh // 2], d[dh // 2 :]
    d_query, d_key, d_value, d_small = all_sum(own, sib, [fq, fk, fk, tail])
    scaled_one = stream * inv_one
    du = n1g * gain_one
    d_tokens = mid_grad + inv_one * (
        du - scaled_one * jnp.mean(du * scaled_one, -1, keepdims=True)
    )
    d_down, d_gate, d_up = (net.shard_sum(v, 0, grads)[None] for v in expert_grads)
    return (
        mixed,
        d_tokens,
        d_small[:, experts + 8],
        d_query,
        d_key,
        d_value,
        d_out,
        d_small[:, experts],
        d_small[:, :experts],
        d_gate,
        d_up,
        d_down,
    )


def solution(mesh):
    rows = P(("dp", "expert"), None)
    flat, dense, routed = P("dp"), P("dp", None), P("expert", "dp", None)
    return jax.shard_map(
        shards,
        mesh=mesh,
        in_specs=(
            rows, rows, rows, rows, flat, dense, dense, dense, dense, flat, dense,
            routed, routed, routed,
        ),
        out_specs=(
            rows, rows, flat, dense, dense, dense, dense, flat, dense, routed, routed, routed,
        ),
        check_vma=False,
    )
```

time: 545 us -> 434 us (0.80)
  waiting for transfers between devices: 204 us -> 150 us
  matrix products: 45.9 us -> 10.5 us
  local copies, waits for them, and re-layouts: 54.6 us -> 22.8 us
  Pallas kernels: 70.7 us -> 102 us
  other arithmetic: 55.5 us -> 32.4 us
  starting transfers between devices: 76.3 us -> 82.1 us
    ppermute x56, waiting for transfers between devices: 143 us -> 101 us  [ring(): return lax.ppermute(v, 'expert', pairs)]
    pallas_call x2 -> x8, Pallas kernels: 22.7 us -> 61.4 us  [the longest x1 14.4 us: projection_gradient(): pl.pallas_call(body, grid_spec=pltpu.PrefetchScalarGridSpec(num_scalar_pr...]
    dot_general x12 -> x0, matrix products: 20.4 us -> none  [the longest x3 8.27 us: mm_nt(): lax.dot_general(a, b, (((1,), (1,)), ((), ())), preferred_element_type=F32)]
    ppermute x16, waiting for transfers between devices: 60.7 us -> 44.5 us  [swap(): return lax.ppermute(v, 'dp', [(0, 1), (1, 0)])]
    unnamed x225 -> x136, local copies, waits for them, and re-layouts: 23.7 us -> 8.71 us
    dot_general x6 -> x3, matrix products: 23.7 us -> 10.5 us  [mm_tn(): lax.dot_general(a, b, (((0,), (0,)), ((), ())), preferred_element_type=F32)]
    ppermute x56, starting transfers between devices: 53.1 us -> 62.3 us  [ring(): return lax.ppermute(v, 'expert', pairs)]
    select_n x4 -> x1, other arithmetic: 7.65 us -> 0.03 us  [both(): jnp.where(self.x == 0, jnp.concatenate([own, got], axis), jnp.concatenate...]
  transfers between devices with their start and end apart: 95 -> 93, of which waited for: 44 -> 41; matrix products, arithmetic and copies ran while one was open for 26% -> 12% of each run, Pallas kernels for 11% -> 19%
where the time goes in v2:
time: 434 us; the launch traced here: 427 us
  waiting for transfers between devices  150 us (35%)
  Pallas kernels  102 us (24%)
  starting transfers between devices  82.1 us (19%)
  other arithmetic  32.4 us (7%)
  between operations  27 us (6%)
  local copies, waits for them, and re-layouts  22.8 us (5%)
  matrix products  10.5 us (2%)
    ppermute x56, waiting for transfers between devices, ring(): return lax.ppermute(v, 'expert', pairs)  101 us
    ppermute x56, starting transfers between devices, ring(): return lax.ppermute(v, 'expert', pairs)  62.3 us
    ppermute x16, waiting for transfers between devices, swap(): return lax.ppermute(v, 'dp', [(0, 1), (1, 0)])  44.5 us
    pallas_call x2, Pallas kernels, expert_step(): pl.pallas_call(body, grid_spec=pltpu.PrefetchScalarGridSpec(num_scalar_pr...  40.7 us
    ppermute x16, starting transfers between devices, swap(): return lax.ppermute(v, 'dp', [(0, 1), (1, 0)])  15.2 us
    pallas_call x1, Pallas kernels, projection_gradient(): pl.pallas_call(body, grid_spec=pltpu.PrefetchScalarGridSpec(num_scalar_pr...  14.4 us
    convert_element_type x26, other arithmetic, narrow(): return v.astype(BF)  13.1 us
    pallas_call x1, Pallas kernels, attend_back(): pl.pallas_call(body, in_specs=[pl.BlockSpec(memory_space=pltpu.SMEM)] + [...  11.7 us
  transfers between devices with their start and end apart: 93, of which 41 were waited for; matrix products, arithmetic and copies ran while one was open for 12% of the time, Pallas kernels for 19%

profile of v2, /device:TPU:0, one launch (start us, length us, event | category | flops | bytes accessed | tf_op | source)
XLA Modules:
  0.0 426.8 jit_solution(3796498801312218219)
XLA Ops:
  27.3 10.2 %collective-permute-done.4.refs_11_.refs_1_ = bf16[192,1536]{1,0:T(8,128)(2,1)} collective-permute-done((bf16[192,1536]{1,0:T(8,128)(2,1)}, bf16[192,1536]{1,0:T(8,128)(2,1)}, u32[]{:S(2)}, u32[]{:S(2)}) %collective-permute-start.4) | collective-permute-done | bytes 589856 | tf_op jit(solution)/shard_map/ppermute | solution.py:678
  42.9 11.4 %project_columns.1 = (f32[128,2560]{1,0:T(8,128)}, bf16[128,2560]{1,0:T(8,128)(2,1)}, bf16[256,768]{1,0:T(8,128)(2,1)}, bf16[768,2560]{1,0:T(8,128)(2,1)}) custom-call(bf16[128,768]{1,0:T(8,128)(2,1)} %get-tuple-element.207.ca, bf16[128,768]{1,0:T(8,128)(2,1)} %collective-permute-done.cb, f32[128,1]{1,0:T(8,128)} %copy.64.ia, f32[128,1]{1,0:T(8,128)} %copy.65.ib, ...), custom_call_target="tpu_custom_call" | custom-call | flops 1006632960 | bytes 11796480 | tf_op jit(solution)/shard_map/project_columns/pallas_call | solution.py:129
  54.6 4.3 %collective-permute-done.5.refs_12_.refs_2_ = bf16[192,1536]{1,0:T(8,128)(2,1)} collective-permute-done((bf16[192,1536]{1,0:T(8,128)(2,1)}, bf16[192,1536]{1,0:T(8,128)(2,1)}, u32[]{:S(2)}, u32[]{:S(2)}) %collective-permute-start.5) | collective-permute-done | bytes 589856 | tf_op jit(solution)/shard_map/ppermute | solution.py:647
  60.4 8.6 %collective-permute-done.2.refs_1_ = bf16[128,2560]{1,0:T(8,128)(2,1)S(1)} collective-permute-done((bf16[128,2560]{1,0:T(8,128)(2,1)}, bf16[128,2560]{1,0:T(8,128)(2,1)S(1)}, u32[]{:S(2)}, u32[]{:S(2)}) %collective-permute-start.2) | collective-permute-done | bytes 655392 | tf_op jit(solution)/shard_map/ppermute | solution.py:678
  72.1 6.6 %attend.1 = (bf16[128,2560]{1,0:T(8,128)(2,1)}, bf16[128,1536]{1,0:T(8,128)(2,1)}, f32[128,1536]{1,0:T(8,128)}, bf16[128,1536]{1,0:T(8,128)(2,1)}, f32[128,128]{1,0:T(8,128)}) custom-call(s32[5]{0:T(128)} %stack.147.spots, f32[128,2560]{1,0:T(8,128)} %get-tuple-element.63.refs_0_, bf16[128,2560]{1,0:T(8,128)(2,1)} %copy-done.33, ...), custom_call_target="tpu_custom_call" | custom-call | flops 805306368 | bytes 8650752 | tf_op jit(solution)/shard_map/attend/pallas_call | solution.py:218
  81.6 6.0 %collective-permute-done.11.refs_4_ = bf16[128,1536]{1,0:T(8,128)(2,1)} collective-permute-done((bf16[128,1536]{1,0:T(8,128)(2,1)}, bf16[128,1536]{1,0:T(8,128)(2,1)}, u32[]{:S(2)}, u32[]{:S(2)}) %collective-permute-start.11) | collective-permute-done | bytes 393248 | tf_op jit(solution)/shard_map/ppermute | solution.py:652
  91.2 8.8 %collective-permute-done.15.refs_8_ = bf16[128,1536]{1,0:T(8,128)(2,1)} collective-permute-done((bf16[128,1536]{1,0:T(8,128)(2,1)}, bf16[128,1536]{1,0:T(8,128)(2,1)}, u32[]{:S(2)}, u32[]{:S(2)}) %collective-permute-start.15) | collective-permute-done | bytes 393248 | tf_op jit(solution)/shard_map/ppermute | solution.py:652
  102.1 4.3 %collective-permute-done.18.refs_13_.refs_11_ = bf16[768,512]{1,0:T(8,128)(2,1)S(1)} collective-permute-done((bf16[768,512]{1,0:T(8,128)(2,1)S(1)}, bf16[768,512]{1,0:T(8,128)(2,1)S(1)}, u32[]{:S(2)}, u32[]{:S(2)}) %collective-permute-start.18) | collective-permute-done | bytes 786464 | tf_op jit(solution)/shard_map/ppermute | solution.py:678
  106.4 12.5 %collective-permute-done.19.refs_15_.refs_13_ = bf16[256,1536]{1,0:T(8,128)(2,1)S(1)} collective-permute-done((bf16[256,1536]{1,0:T(8,128)(2,1)S(1)}, bf16[256,1536]{1,0:T(8,128)(2,1)S(1)}, u32[]{:S(2)}, u32[]{:S(2)}) %collective-permute-start.19) | collective-permute-done | bytes 786464 | tf_op jit(solution)/shard_map/ppermute | solution.py:678
  138.4 23.9 %expert_step.2 = (bf16[640,1536]{1,0:T(8,128)(2,1)}, bf16[640,1536]{1,0:T(8,128)(2,1)}, bf16[640,1664]{1,0:T(8,128)(2,1)}, bf16[640,1664]{1,0:T(8,128)(2,1)}, bf...) custom-call(s32[11]{0:T(128)} %stack.159.spot, ...), custom_call_target="tpu_custom_call" | custom-call | flops 12079595520 | bytes 32243712 | tf_op jit(solution)/shard_map/expert_step/pallas_call | solution.py:584
  163.4 16.7 %expert_step.3 = (bf16[384,1536]{1,0:T(8,128)(2,1)}, bf16[384,1536]{1,0:T(8,128)(2,1)}, bf16[384,1664]{1,0:T(8,128)(2,1)}, bf16[384,1664]{1,0:T(8,128)(2,1)}, bf...) custom-call(s32[7]{0:T(128)} %stack.170.spot, ...), custom_call_target="tpu_custom_call", output_to_operand_aliasing={{4}: (19, {}), {5}: (20, {}), {6}: (21, {}), {7}: (22, {}),... | custom-call | flops 7247757312 | bytes 21233664 | tf_op jit(solution)/shard_map/expert_step/pallas_call | solution.py:584
  188.9 5.7 %collective-permute-done.31 = bf16[64,1664]{1,0:T(8,128)(2,1)S(1)} collective-permute-done((bf16[64,1664]{1,0:T(8,128)(2,1)S(1)}, bf16[64,1664]{1,0:T(8,128)(2,1)S(1)}, u32[]{:S(2)}, u32[]{:S(2)}) %collective-permute-start.31) | collective-permute-done | bytes 213024 | tf_op jit(solution)/shard_map/ppermute | solution.py:652
  197.4 3.5 fusion.36
  201.1 3.5 fusion.34
  209.5 3.5 fusion.35
  213.3 3.9 collective-permute-done.46
  222.3 5.6 %collective-permute-done.35.b = bf16[128,1664]{1,0:T(8,128)(2,1)S(1)} collective-permute-done((bf16[128,1664]{1,0:T(8,128)(2,1)S(1)}, bf16[128,1664]{1,0:T(8,128)(2,1)S(1)}, u32[]{:S(2)}, u32[]{:S(2)}) %collective-permute-start.35) | collective-permute-done | bytes 426016 | tf_op jit(solution)/shard_map/ppermute | solution.py:652
  229.9 6.3 %collective-permute-done.47.c = bf16[128,1664]{1,0:T(8,128)(2,1)S(1)} collective-permute-done((bf16[128,1664]{1,0:T(8,128)(2,1)S(1)}, bf16[128,1664]{1,0:T(8,128)(2,1)S(1)}, u32[]{:S(2)}, u32[]{:S(2)}) %collective-permute-start.47) | collective-permute-done | bytes 426016 | tf_op jit(solution)/shard_map/ppermute | solution.py:652
  236.9 3.6 second_norm_back.1
  240.9 11.7 %attend_back.1.ga = bf16[128,2560]{1,0:T(8,128)(2,1)} custom-call(s32[5]{0:T(128)} %stack.147.spots, bf16[128,2560]{1,0:T(8,128)(2,1)} %get-tuple-element.86.qkv_r, f32[128,128]{1,0:T(8,128)} %get-tuple-element.211.refs_2_.cosine, f32[128,128]{1,0:T(8,128)} %get-tuple-element.210.refs_3_.sine, f32[128,128]{1,0:T(8,128)} %fusion.12.refs_4_.allowed, ...), custom_call_target="tpu_custom_call" | custom-call | flops 1207959552 | bytes 7340032 | tf_op jit(solution)/shard_map/attend_back/pallas_call | solution.py:331
  263.5 3.9 collective-permute-done.70.bb
  267.4 3.7 out_gradient.1
  280.4 14.4 %projection_gradient.1 = (bf16[384,2688]{1,0:T(8,128)(2,1)}, bf16[384,2688]{1,0:T(8,128)(2,1)}, f32[128,768]{1,0:T(8,128)}, bf16[128,768]{1,0:T(8,128)(2,1)}) custom-call(s32[16]{0:T(128)} %stack.187.at.at_ref, bf16[128,2560]{1,0:T(8,128)(2,1)} %attend_back.1.ga, bf16[128,2560]{1,0:T(8,128)(2,1)} %collective-permute-done.48.gb, ...), custom_call_target="tpu_custom_call" | custom-call | flops 2013265920 | bytes 7864320 | tf_op jit(solution)/shard_map/projection_gradient/pallas_call | solution.py:419
  307.1 5.3 %collective-permute-done.73 = bf16[48,1536]{1,0:T(8,128)(2,1)S(1)} collective-permute-done((bf16[48,1536]{1,0:T(8,128)(2,1)S(1)}, bf16[48,1536]{1,0:T(8,128)(2,1)S(1)}, u32[]{:S(2)}, u32[]{:S(2)}) %collective-permute-start.73) | collective-permute-done | bytes 147488 | tf_op jit(solution)/shard_map/ppermute | solution.py:652
  338.4 4.5 %collective-permute-done.84 = bf16[48,1536]{1,0:T(8,128)(2,1)S(1)} collective-permute-done((bf16[48,1536]{1,0:T(8,128)(2,1)S(1)}, bf16[48,1536]{1,0:T(8,128)(2,1)S(1)}, u32[]{:S(2)}, u32[]{:S(2)}) %collective-permute-start.84) | collective-permute-done | bytes 147488 | tf_op jit(solution)/shard_map/ppermute | solution.py:652
  358.7 5.9 %collective-permute-done.87 = bf16[24,1536]{1,0:T(8,128)(2,1)S(1)} collective-permute-done((bf16[24,1536]{1,0:T(8,128)(2,1)S(1)}, bf16[24,1536]{1,0:T(8,128)(2,1)S(1)}, u32[]{:S(2)}, u32[]{:S(2)}) %collective-permute-start.87) | collective-permute-done | bytes 73760 | tf_op jit(solution)/shard_map/ppermute | solution.py:652
  370.0 3.6 collective-permute-done.64
  381.6 3.7 collective-permute-done.62
  385.8 4.5 %collective-permute-done.67 = bf16[24,2688]{1,0:T(8,128)(2,1)S(1)} collective-permute-done((bf16[24,2688]{1,0:T(8,128)(2,1)S(1)}, bf16[24,2688]{1,0:T(8,128)(2,1)S(1)}, u32[]{:S(2)}, u32[]{:S(2)}) %collective-permute-start.67) | collective-permute-done | bytes 129056 | tf_op jit(solution)/shard_map/ppermute | solution.py:652
  394.7 7.8 %collective-permute-done.39 = bf16[128,1536]{1,0:T(8,128)(2,1)S(1)} collective-permute-done((bf16[128,1536]{1,0:T(8,128)(2,1)S(1)}, bf16[128,1536]{1,0:T(8,128)(2,1)S(1)}, u32[]{:S(2)}, u32[]{:S(2)}) %collective-permute-start.39) | collective-permute-done | bytes 393248 | tf_op jit(solution)/shard_map/ppermute | solution.py:652
  404.4 4.0 put_rows.3
  409.7 6.0 %put_rows.2 = (f32[768,1536]{1,0:T(8,128)}, f32[768,512]{1,0:T(8,128)}, f32[768,512]{1,0:T(8,128)}, f32[768,128]{1,0:T(8,128)}) custom-call(s32[16]{0:T(128)} %stack.187.at.at_ref, bf16[384,2688]{1,0:T(8,128)(2,1)} %copy-done.9, bf16[384,2688]{1,0:T(8,128)(2,1)} %copy-done.17), custom_call_target="tpu_custom_call" | custom-call | flops 2064384 | bytes 12386304 | tf_op jit(solution)/shard_map/put_rows/pallas_call | solution.py:473
  (408 shorter events, 171.7 us)
Async XLA Ops:
  7.2 131.2 %all-gather.2.cloned.1.call-start = ((), (), s32[]{:S(2)}) async-start(), calls=%async_computation | async-start | bytes 7241728 | tf_op jit(solution)/shard_map/all_gather | solution.py:792
  11.3 30.8 %collective-permute-start.1 = (f32[1,128]{1,0:T(1,128)S(1)}, f32[1,128]{1,0:T(1,128)S(1)}, u32[]{:S(2)}, u32[]{:S(2)}) collective-permute-start(f32[1,128]{1,0:T(1,128)S(1)} %fusion.43), channel_id=1, source_target_pairs={{0,16},{16,0},{1,17},{17,1},{2,18},{18,2},{3,19},{19,3},{4,20},{20... | collective-permute-start | bytes 1544 | tf_op jit(solution)/shard_map/ppermute | solution.py:678
  16.6 42.4 %collective-permute-start.3 = (bf16[18,768]{1,0:T(8,128)(2,1)S(1)}, bf16[18,768]{1,0:T(8,128)(2,1)S(1)}, u32[]{:S(2)}, u32[]{:S(2)}) collective-permute-start(bf16[18,768]{1,0:T(8,128)(2,1)S(1)} %pad_maximum_fusion.9), channel_id=1, source_target_pairs={{0,16},{16,0},{1,17},{17,1},{2,18},{18,2},{3,19},{19,3},{4,20},{20... | collective-permute-start | bytes 82952 | tf_op jit(solution)/shard_map/ppermute | solution.py:678
  17.4 25.5 %collective-permute-start = (bf16[128,768]{1,0:T(8,128)(2,1)S(1)}, bf16[128,768]{1,0:T(8,128)(2,1)}, u32[]{:S(2)}, u32[]{:S(2)}) collective-permute-start(bf16[128,768]{1,0:T(8,128)(2,1)S(1)} %get-tuple-element.206), channel_id=1, source_target_pairs={{0,16},{16,0},{1,17},{17,1},{2,18},{18,2},{3,19},{19,3},{4,20},{20... | collective-permute-start | bytes 589832 | tf_op jit(solution)/shard_map/ppermute | solution.py:678
  37.5 21.4 %collective-permute-start.5 = (bf16[192,1536]{1,0:T(8,128)(2,1)}, bf16[192,1536]{1,0:T(8,128)(2,1)}, u32[]{:S(2)}, u32[]{:S(2)}) collective-permute-start(bf16[192,1536]{1,0:T(8,128)(2,1)} %collective-permute-done.4.refs_11_.refs_1_), channel_id=1, source_target_pairs={{0,2},{1,3},{2,0},{3,1},{4,6},{5,7},{6,4},{7,5},{8,10},{9,11},{10,... | collective-permute-start | bytes 1769480 | tf_op jit(solution)/shard_map/ppermute | solution.py:647
  69.0 33.0 %collective-permute-start.17 = (bf16[768,512]{1,0:T(8,128)(2,1)S(1)}, bf16[768,512]{1,0:T(8,128)(2,1)S(1)}, u32[]{:S(2)}, u32[]{:S(2)}) collective-permute-start(bf16[768,512]{1,0:T(8,128)(2,1)S(1)} %convert_bitcast_fusion.2.refs_10_.refs_8_), channel_id=1, source_target_pairs={{0,16},{16,0},{1,17},{17,1},{2,18},{18,2},{3,19},{19,3},{4,20},{20... | collective-permute-start | bytes 2359304 | tf_op jit(solution)/shard_map/ppermute | solution.py:678
  69.7 36.7 %collective-permute-start.18 = (bf16[768,512]{1,0:T(8,128)(2,1)S(1)}, bf16[768,512]{1,0:T(8,128)(2,1)S(1)}, u32[]{:S(2)}, u32[]{:S(2)}) collective-permute-start(bf16[768,512]{1,0:T(8,128)(2,1)S(1)} %copy-done.7), channel_id=1, source_target_pairs={{0,16},{16,0},{1,17},{17,1},{2,18},{18,2},{3,19},{19,3},{4,20},{20... | collective-permute-start | bytes 2359304 | tf_op jit(solution)/shard_map/ppermute | solution.py:678
  80.9 38.0 %collective-permute-start.19 = (bf16[256,1536]{1,0:T(8,128)(2,1)S(1)}, bf16[256,1536]{1,0:T(8,128)(2,1)S(1)}, u32[]{:S(2)}, u32[]{:S(2)}) collective-permute-start(bf16[256,1536]{1,0:T(8,128)(2,1)S(1)} %convert_bitcast_fusion.refs_14_.refs_12_), channel_id=1, source_target_pairs={{0,16},{16,0},{1,17},{17,1},{2,18},{18,2},{3,19},{19,3},{4,20},{20... | collective-permute-start | bytes 2359304 | tf_op jit(solution)/shard_map/ppermute | solution.py:678
  100.0 19.0 %collective-permute-start.21 = (bf16[128,1536]{1,0:T(8,128)(2,1)}, bf16[128,1536]{1,0:T(8,128)(2,1)S(1)}, u32[]{:S(2)}, u32[]{:S(2)}) collective-permute-start(bf16[128,1536]{1,0:T(8,128)(2,1)} %collective-permute-done.15.refs_8_), channel_id=1, source_target_pairs={{0,4},{1,5},{4,8},{5,9},{8,12},{9,13},{12,14},{13,15},{14,10},{15,... | collective-permute-start | bytes 1179656 | tf_op jit(solution)/shard_map/ppermute | solution.py:652
  100.0 19.5 %collective-permute-start.23 = (bf16[128,1536]{1,0:T(8,128)(2,1)}, bf16[128,1536]{1,0:T(8,128)(2,1)S(1)}, u32[]{:S(2)}, u32[]{:S(2)}) collective-permute-start(bf16[128,1536]{1,0:T(8,128)(2,1)} %collective-permute-done.13.refs_6_), channel_id=1, source_target_pairs={{0,2},{1,3},{4,0},{5,1},{8,4},{9,5},{12,8},{13,9},{14,12},{15,13},... | collective-permute-start | bytes 1179656 | tf_op jit(solution)/shard_map/ppermute | solution.py:652
  118.9 18.1 %collective-permute-start.10 = (bf16[128,1536]{1,0:T(8,128)(2,1)}, bf16[128,1536]{1,0:T(8,128)(2,1)S(1)}, u32[]{:S(2)}, u32[]{:S(2)}) collective-permute-start(bf16[128,1536]{1,0:T(8,128)(2,1)} %collective-permute-done.9.refs_2_), channel_id=1, source_target_pairs={{0,1},{1,0},{2,3},{3,2},{4,5},{5,4},{6,7},{7,6},{8,9},{9,8},{10,11... | collective-permute-start | bytes 1179656 | tf_op jit(solution)/shard_map/ppermute | solution.py:644
  118.9 18.8 %collective-permute-start.16 = (bf16[128,1536]{1,0:T(8,128)(2,1)}, bf16[128,1536]{1,0:T(8,128)(2,1)}, u32[]{:S(2)}, u32[]{:S(2)}) collective-permute-start(bf16[128,1536]{1,0:T(8,128)(2,1)} %collective-permute-done.15.refs_8_), channel_id=1, source_target_pairs={{0,1},{1,0},{2,3},{3,2},{4,5},{5,4},{6,7},{7,6},{8,9},{9,8},{10,11... | collective-permute-start | bytes 1179656 | tf_op jit(solution)/shard_map/ppermute | solution.py:644
  119.8 18.6 %collective-permute-start.14 = (bf16[128,1536]{1,0:T(8,128)(2,1)}, bf16[128,1536]{1,0:T(8,128)(2,1)}, u32[]{:S(2)}, u32[]{:S(2)}) collective-permute-start(bf16[128,1536]{1,0:T(8,128)(2,1)} %collective-permute-done.13.refs_6_), channel_id=1, source_target_pairs={{0,1},{1,0},{2,3},{3,2},{4,5},{5,4},{6,7},{7,6},{8,9},{9,8},{10,11... | collective-permute-start | bytes 1179656 | tf_op jit(solution)/shard_map/ppermute | solution.py:644
  137.0 25.4 %collective-permute-start.28 = (bf16[128,1536]{1,0:T(8,128)(2,1)S(1)}, bf16[128,1536]{1,0:T(8,128)(2,1)S(1)}, u32[]{:S(2)}, u32[]{:S(2)}) collective-permute-start(bf16[128,1536]{1,0:T(8,128)(2,1)S(1)} %collective-permute-done.21.refs_6_), channel_id=1, source_target_pairs={{0,1},{1,0},{2,3},{3,2},{4,5},{5,4},{6,7},{7,6},{8,9},{9,8},{10,11... | collective-permute-start | bytes 1179656 | tf_op jit(solution)/shard_map/ppermute | solution.py:644
  137.8 24.6 %collective-permute-start.27 = (bf16[128,1536]{1,0:T(8,128)(2,1)S(1)}, bf16[128,1536]{1,0:T(8,128)(2,1)S(1)}, u32[]{:S(2)}, u32[]{:S(2)}) collective-permute-start(bf16[128,1536]{1,0:T(8,128)(2,1)S(1)} %collective-permute-done.23.refs_4_), channel_id=1, source_target_pairs={{0,1},{1,0},{2,3},{3,2},{4,5},{5,4},{6,7},{7,6},{8,9},{9,8},{10,11... | collective-permute-start | bytes 1179656 | tf_op jit(solution)/shard_map/ppermute | solution.py:644
  137.8 24.6 %collective-permute-start.25 = (bf16[64,1536]{1,0:T(8,128)(2,1)S(1)}, bf16[64,1536]{1,0:T(8,128)(2,1)S(1)}, u32[]{:S(2)}, u32[]{:S(2)}) collective-permute-start(bf16[64,1536]{1,0:T(8,128)(2,1)S(1)} %collective-permute-done.22.refs_0_), channel_id=1, source_target_pairs={{0,1},{1,0},{2,3},{3,2},{4,5},{5,4},{6,7},{7,6},{8,9},{9,8},{10,11... | collective-permute-start | bytes 589832 | tf_op jit(solution)/shard_map/ppermute | solution.py:644
  138.3 24.1 %collective-permute-start.26 = (bf16[64,1536]{1,0:T(8,128)(2,1)S(1)}, bf16[64,1536]{1,0:T(8,128)(2,1)S(1)}, u32[]{:S(2)}, u32[]{:S(2)}) collective-permute-start(bf16[64,1536]{1,0:T(8,128)(2,1)S(1)} %collective-permute-done.24.refs_1_), channel_id=1, source_target_pairs={{0,1},{1,0},{2,3},{3,2},{4,5},{5,4},{6,7},{7,6},{8,9},{9,8},{10,11... | collective-permute-start | bytes 589832 | tf_op jit(solution)/shard_map/ppermute | solution.py:644
  183.0 79.8 %collective-permute-start.69 = (bf16[128,768]{1,0:T(8,128)(2,1)}, bf16[128,768]{1,0:T(8,128)(2,1)}, u32[]{:S(2)}, u32[]{:S(2)}) collective-permute-start(bf16[128,768]{1,0:T(8,128)(2,1)} %get-tuple-element.100), channel_id=1, source_target_pairs={{0,16},{16,0},{1,17},{17,1},{2,18},{18,2},{3,19},{19,3},{4,20},{20... | collective-permute-start | bytes 589832 | tf_op jit(solution)/shard_map/ppermute | solution.py:678
  184.1 35.4 %collective-permute-start.20 = (bf16[640,1536]{1,0:T(8,128)(2,1)}, bf16[640,1536]{1,0:T(8,128)(2,1)S(1)}, u32[]{:S(2)}, u32[]{:S(2)}) collective-permute-start(bf16[640,1536]{1,0:T(8,128)(2,1)} %get-tuple-element.71), channel_id=1, source_target_pairs={{0,1},{1,0},{2,3},{3,2},{4,5},{5,4},{6,7},{7,6},{8,9},{9,8},{10,11... | collective-permute-start | bytes 5898248 | tf_op jit(solution)/shard_map/ppermute | solution.py:644
  184.3 20.3 %collective-permute-start.33 = (bf16[640,1664]{1,0:T(8,128)(2,1)}, bf16[640,1664]{1,0:T(8,128)(2,1)S(1)}, u32[]{:S(2)}, u32[]{:S(2)}) collective-permute-start(bf16[640,1664]{1,0:T(8,128)(2,1)} %get-tuple-element.82), channel_id=1, source_target_pairs={{0,1},{1,0},{2,3},{3,2},{4,5},{5,4},{6,7},{7,6},{8,9},{9,8},{10,11... | collective-permute-start | bytes 6389768 | tf_op jit(solution)/shard_map/ppermute | solution.py:644
  204.6 48.0 %collective-permute-start.91 = (bf16[256,1536]{1,0:T(8,128)(2,1)S(1)}, bf16[256,1536]{1,0:T(8,128)(2,1)}, u32[]{:S(2)}, u32[]{:S(2)}) collective-permute-start(bf16[256,1536]{1,0:T(8,128)(2,1)S(1)} %dynamic-slice_convert_fusion), channel_id=1, source_target_pairs={{0,16},{16,0},{1,17},{17,1},{2,18},{18,2},{3,19},{19,3},{4,20},{20... | collective-permute-start | bytes 2359304 | tf_op jit(solution)/shard_map/ppermute | solution.py:678
  217.2 40.8 %collective-permute-start.89 = (bf16[768,512]{1,0:T(8,128)(2,1)S(1)}, bf16[768,512]{1,0:T(8,128)(2,1)}, u32[]{:S(2)}, u32[]{:S(2)}) collective-permute-start(bf16[768,512]{1,0:T(8,128)(2,1)S(1)} %dynamic-slice_convert_fusion.2), channel_id=1, source_target_pairs={{0,16},{16,0},{1,17},{17,1},{2,18},{18,2},{3,19},{19,3},{4,20},{20... | collective-permute-start | bytes 2359304 | tf_op jit(solution)/shard_map/ppermute | solution.py:678
  217.7 41.3 %collective-permute-start.90 = (bf16[768,512]{1,0:T(8,128)(2,1)S(1)}, bf16[768,512]{1,0:T(8,128)(2,1)}, u32[]{:S(2)}, u32[]{:S(2)}) collective-permute-start(bf16[768,512]{1,0:T(8,128)(2,1)S(1)} %dynamic-slice_convert_fusion.1), channel_id=1, source_target_pairs={{0,16},{16,0},{1,17},{17,1},{2,18},{18,2},{3,19},{19,3},{4,20},{20... | collective-permute-start | bytes 2359304 | tf_op jit(solution)/shard_map/ppermute | solution.py:678
  240.6 26.9 %collective-permute-start.70 = (bf16[128,1536]{1,0:T(8,128)(2,1)}, bf16[128,1536]{1,0:T(8,128)(2,1)}, u32[]{:S(2)}, u32[]{:S(2)}) collective-permute-start(bf16[128,1536]{1,0:T(8,128)(2,1)} %get-tuple-element.87.br.ba), channel_id=1, source_target_pairs={{0,16},{16,0},{1,17},{17,1},{2,18},{18,2},{3,19},{19,3},{4,20},{20... | collective-permute-start | bytes 1179656 | tf_op jit(solution)/shard_map/ppermute | solution.py:678
  252.6 27.2 %collective-permute-start.48 = (bf16[128,2560]{1,0:T(8,128)(2,1)}, bf16[128,2560]{1,0:T(8,128)(2,1)}, u32[]{:S(2)}, u32[]{:S(2)}) collective-permute-start(bf16[128,2560]{1,0:T(8,128)(2,1)} %attend_back.1.ga), channel_id=1, source_target_pairs={{0,16},{16,0},{1,17},{17,1},{2,18},{18,2},{3,19},{19,3},{4,20},{20... | collective-permute-start | bytes 1966088 | tf_op jit(solution)/shard_map/ppermute | solution.py:678
  258.0 21.9 %collective-permute-start.49 = (bf16[32,768]{1,0:T(8,128)(2,1)S(1)}, bf16[32,768]{1,0:T(8,128)(2,1)S(1)}, u32[]{:S(2)}, u32[]{:S(2)}) collective-permute-start(bf16[32,768]{1,0:T(8,128)(2,1)S(1)} %get-tuple-element.208), channel_id=1, source_target_pairs={{0,16},{16,0},{1,17},{17,1},{2,18},{18,2},{3,19},{19,3},{4,20},{20... | collective-permute-start | bytes 147464 | tf_op jit(solution)/shard_map/ppermute | solution.py:678
  271.1 24.4 %collective-permute-start.71 = (bf16[384,1536]{1,0:T(8,128)(2,1)}, bf16[384,1536]{1,0:T(8,128)(2,1)S(1)}, u32[]{:S(2)}, u32[]{:S(2)}) collective-permute-start(bf16[384,1536]{1,0:T(8,128)(2,1)} %get-tuple-element.102), channel_id=1, source_target_pairs={{0,1},{1,0},{2,3},{3,2},{4,5},{5,4},{6,7},{7,6},{8,9},{9,8},{10,11... | collective-permute-start | bytes 3538952 | tf_op jit(solution)/shard_map/ppermute | solution.py:644
  274.4 23.0 %collective-permute-start.41 = (bf16[128,1536]{1,0:T(8,128)(2,1)S(1)}, bf16[128,1536]{1,0:T(8,128)(2,1)S(1)}, u32[]{:S(2)}, u32[]{:S(2)}) collective-permute-start(bf16[128,1536]{1,0:T(8,128)(2,1)S(1)} %pad_maximum_fusion.4), channel_id=1, source_target_pairs={{0,2},{1,3},{4,0},{5,1},{8,4},{9,5},{12,8},{13,9},{14,12},{15,13},... | collective-permute-start | bytes 1179656 | tf_op jit(solution)/shard_map/ppermute | solution.py:652
  275.9 22.1 %collective-permute-start.37 = (bf16[128,1536]{1,0:T(8,128)(2,1)S(1)}, bf16[128,1536]{1,0:T(8,128)(2,1)S(1)}, u32[]{:S(2)}, u32[]{:S(2)}) collective-permute-start(bf16[128,1536]{1,0:T(8,128)(2,1)S(1)} %pad_maximum_fusion.3), channel_id=1, source_target_pairs={{0,4},{1,5},{4,8},{5,9},{8,12},{9,13},{12,14},{13,15},{14,10},{15,... | collective-permute-start | bytes 1179656 | tf_op jit(solution)/shard_map/ppermute | solution.py:652
  295.6 19.2 %collective-permute-start.51 = (bf16[384,2688]{1,0:T(8,128)(2,1)}, bf16[384,2688]{1,0:T(8,128)(2,1)S(1)}, u32[]{:S(2)}, u32[]{:S(2)}) collective-permute-start(bf16[384,2688]{1,0:T(8,128)(2,1)} %get-tuple-element.94), channel_id=1, source_target_pairs={{0,1},{1,0},{2,3},{3,2},{4,5},{5,4},{6,7},{7,6},{8,9},{9,8},{10,11... | collective-permute-start | bytes 6193160 | tf_op jit(solution)/shard_map/ppermute | solution.py:644
  298.2 93.0 %collective-permute-start.38 = (bf16[128,1536]{1,0:T(8,128)(2,1)S(1)}, bf16[128,1536]{1,0:T(8,128)(2,1)S(1)}, u32[]{:S(2)}, u32[]{:S(2)}) collective-permute-start(bf16[128,1536]{1,0:T(8,128)(2,1)S(1)} %get-tuple-element.180), channel_id=1, source_target_pairs={{0,4},{1,5},{4,8},{5,9},{8,12},{9,13},{12,14},{13,15},{14,10},{15,... | collective-permute-start | bytes 1179656 | tf_op jit(solution)/shard_map/ppermute | solution.py:652
  349.0 42.2 %collective-permute-start.42 = (bf16[128,1536]{1,0:T(8,128)(2,1)S(1)}, bf16[128,1536]{1,0:T(8,128)(2,1)S(1)}, u32[]{:S(2)}, u32[]{:S(2)}) collective-permute-start(bf16[128,1536]{1,0:T(8,128)(2,1)S(1)} %get-tuple-element.181), channel_id=1, source_target_pairs={{0,2},{1,3},{4,0},{5,1},{8,4},{9,5},{12,8},{13,9},{14,12},{15,13},... | collective-permute-start | bytes 1179656 | tf_op jit(solution)/shard_map/ppermute | solution.py:652
  (122 other events, 1314.8 us)
Sparse Core Ops, SparseCore 0:
  10.9 73.7 all-gather.1
